TPU v7x, 512 devices: a whole 4x8x8 slice. The times are simulated.
512 devices in a mesh: band: 16 (over y, core), ga: 32 (over z, x).
Axes of the slice: x: 4, y: 8, z: 8, core: 2. Of those that a mesh axis runs over, the one named last changes fastest.
Arguments:
- coef_x: float32 [16, 3072, 256], P('band', 'ga'), may hold values from -26 to 26
- coef_w: float32 [16, 3072, 256], P('band', 'ga'), may hold values from -26 to 26
- coef_p: float32 [16, 3072, 256], P('band', 'ga'), may hold values from -26 to 26
- hcoef_x: float32 [16, 3072, 256], P('band', 'ga'), may hold values from -110 to 110
- hcoef_p: float32 [16, 3072, 256], P('band', 'ga'), may hold values from -110 to 110
- potential: float32 [128, 128, 128], P('ga'), may hold values from -5 to 5
- stick_column: int32 [3072], replicated, may hold values from 0 to 16383, as said below
- sphere_mask: int32 [3072, 128], P('ga'), may hold values from 0 to 1, as said below
Outputs:
- h_wave: float32 [16, 3072, 256], P('band', 'ga')
- reduced: float32 [96, 96], replicated
Inputs may be any that keep to these rules, and one draw needn't show every extreme that they name: `stick_column`: distinct grid columns: the 3072 columns of smallest f(y)^2 + f(z)^2, ties on the outermost circle broken at random, in random order. `sphere_mask`: a sphere: ones exactly where f(k)^2 + f(y_s)^2 + f(z_s)^2 is at most the largest f(y_s)^2 + f(z_s)^2 over all sticks.
All inputs are finite; a program needn't handle non-finite values.
Results may differ from a plain program's by a relative error of at most 0.00012.
Values sent between devices are 32-bit elements; how exact they have to be, the bound alone decides.
A program may use at most 128 MiB of HBM per device.

v0:
```python
import math

import jax
import jax.numpy as jnp
from jax import lax
from jax.sharding import PartitionSpec as P


def folded(count):
    k = jnp.arange(count, dtype=jnp.int32)
    return jnp.where(k < count // 2, k, k - count)


def dft_tables(count):
    k = jnp.arange(count, dtype=jnp.int32)
    phase = (k[:, None] * k[None, :] % count).astype(jnp.float32) * (2.0 * math.pi / count)
    return (jnp.cos(phase), jnp.sin(phase))


def complex_table(cosine, sine, sign):
    real_row = jnp.stack([cosine, sign * sine], axis=1)
    imag_row = jnp.stack([-sign * sine, cosine], axis=1)
    return jnp.stack([real_row, imag_row], axis=0)


def turn_axis(field, table, form):
    return jnp.einsum(form, field, table, precision=lax.Precision.HIGHEST)


def turned(v, count):
    return jnp.concatenate([v[..., count:], -v[..., :count]], axis=-1)


def shards(coef_x, coef_w, coef_p, hcoef_x, hcoef_p, potential, stick_column, sphere_mask):
    hi = lax.Precision.HIGHEST
    count = potential.shape[1]
    planes_dev = potential.shape[0]
    sticks_dev = sphere_mask.shape[0]
    bands_dev = coef_w.shape[0]
    groups = lax.axis_size("band")
    cosine, sine = dft_tables(count)
    forward_table = jnp.block([[cosine, sine], [-sine, cosine]])
    inverse_table = jnp.block([[cosine, -sine], [sine, cosine]])
    plus_table = complex_table(cosine, sine, 1.0)
    minus_table = complex_table(cosine, sine, -1.0)
    mine = lax.dynamic_slice_in_dim(stick_column, lax.axis_index("ga") * sticks_dev, sticks_dev)
    fx = folded(count).astype(jnp.float32)
    fy = folded(count)[mine // count].astype(jnp.float32)
    fz = folded(count)[mine % count].astype(jnp.float32)
    kinetic = 0.5 * (2.0 * math.pi / count) ** 2 * (fx[None, :] ** 2 + (fy**2 + fz**2)[:, None])
    kin_two = jnp.concatenate([kinetic, kinetic], axis=1)
    maskf = sphere_mask.astype(jnp.float32)
    mask_two = jnp.concatenate([maskf, maskf], axis=1)
    w_masked = coef_w * mask_two[None]
    along_x = jnp.einsum("bsk,kx->bsx", w_masked, forward_table, precision=hi)
    along_x = along_x.reshape(bands_dev, sticks_dev, 2, count)
    block = lax.all_to_all(along_x, "ga", split_axis=3, concat_axis=1, tiled=True)
    items = block.shape[0]
    values = jnp.transpose(block, (0, 3, 2, 1))
    grid = jnp.zeros((items, planes_dev, 2, count * count), jnp.float32)
    grid = grid.at[..., stick_column].set(values).reshape(items, planes_dev, 2, count, count)
    grid = turn_axis(grid, plus_table, "npcyz,czdw->npdyw")
    grid = turn_axis(grid, plus_table, "npcyz,cydw->npdwz")
    grid = grid * potential[None, :, None]
    grid = turn_axis(grid, minus_table, "npcyz,czdw->npdyw")
    grid = turn_axis(grid, minus_table, "npcyz,cydw->npdwz")
    grid = grid * (1.0 / float(count) ** 3)
    picked = grid.reshape(items, planes_dev, 2, count * count)[..., stick_column]
    picked = jnp.transpose(picked, (0, 3, 2, 1))
    returned = lax.all_to_all(picked, "ga", split_axis=1, concat_axis=3, tiled=True)
    returned = returned.reshape(bands_dev, sticks_dev, 2 * count)
    local_part = jnp.einsum("bsk,kx->bsx", returned, inverse_table, precision=hi)
    h_wave = mask_two[None] * (kin_two[None] * w_masked + local_part)
    span = jnp.stack([coef_x * mask_two[None], w_masked, coef_p * mask_two[None]])
    image = jnp.stack([hcoef_x * mask_two[None], h_wave, hcoef_p * mask_two[None]])
    bands = bands_dev * groups
    width = 3 * bands
    own_cols = jnp.stack([image, turned(image, count), span, turned(span, count)])
    own_cols = own_cols.reshape(12 * bands_dev, -1)
    empty = jnp.zeros((3, bands, 4, 3 * bands_dev), jnp.float32)
    piece = lax.all_gather(span, "band", axis=1, tiled=True)
    rows = piece.shape[1]
    flat = piece.reshape(3 * rows, -1)
    product = jnp.einsum("il,jl->ij", flat, own_cols, precision=hi)
    product = product.reshape(3, rows, 4, 3 * bands_dev)
    columns = lax.dynamic_update_slice_in_dim(empty, empty + product, jnp.int32(0), 1)
    summed = lax.psum(columns, "ga")
    whole = lax.all_gather(summed, "band", axis=3, tiled=True)
    whole = whole.reshape(3, bands, 4, groups, 3, bands_dev)
    whole = jnp.transpose(whole, (2, 0, 1, 4, 3, 5)).reshape(4, width, width)
    big_h = jnp.block([[whole[0], -whole[1]], [whole[1], whole[0]]])
    big_s = jnp.block([[whole[2], -whole[3]], [whole[3], whole[2]]])
    lower = jnp.linalg.cholesky(big_s)
    first = jax.scipy.linalg.solve_triangular(lower, big_h, lower=True)
    reduced = jax.scipy.linalg.solve_triangular(lower, first.T, lower=True).T
    return (h_wave, reduced)


def solution(mesh):
    in_specs = (
        P("band", "ga", None),
        P("band", "ga", None),
        P("band", "ga", None),
        P("band", "ga", None),
        P("band", "ga", None),
        P("ga", None, None),
        P(),
        P("ga", None),
    )
    out_specs = (P("band", "ga", None), P())
    return jax.shard_map(shards, mesh=mesh, in_specs=in_specs, out_specs=out_specs, check_vma=False)
```

profile of v0, /device:TPU:1, one launch (start us, length us, event | category | flops | bytes accessed | tf_op | source)
XLA Modules:
  0.0 627.6 jit_solution(2901395726915285962)
XLA Ops:
  7.2 0.8 convert_element_type.72
  8.0 1.1 fusion.40
  9.2 0.8 pad_maximum_fusion.4
  10.0 0.3 fusion.73
  10.3 0.3 fusion.69
  10.7 0.3 copy-done.9
  10.9 0.4 convolution_bitcast_fusion.4
  11.3 0.8 copy.78
  12.1 13.7 %all-to-all-start = ((f32[1,96,2,128]{1,2,0,3:T(2,128)}), f32[1,96,2,128]{1,2,0,3:T(2,128)S(1)}, u32[]{:S(2)}, u32[]{:S(2)}) async-start(f32[1,96,2,128]{1,2,0,3:T(2,128)} %copy.78), calls=%async_computation | async-start | bytes 262144 | tf_op jit(solution)/shard_map/all_to_all | solution.py:57
  25.8 0.8 stack.113
  26.6 0.7 stack.112
  27.3 0.7 stack.114
  28.1 0.1 compare_select_fusion.2
  28.2 1.2 gather_fusion.1
  29.4 1.2 gather_fusion
  30.7 1.1 stack.116
  31.8 0.7 stack.103
  32.5 0.7 stack.105
  33.3 0.3 fusion.72
  33.6 0.3 broadcast_multiply_fusion
  33.8 0.7 fusion.37
  34.6 0.6 all-to-all-done
  35.2 0.8 all_to_all.27
  36.0 3.8 copy.81
  39.8 6.1 broadcast.214
  45.8 280.1 %scatter_fusion = f32[4,2,16384]{0,1,2:T(2,128)} fusion(f32[4,2,16384]{0,1,2:T(2,128)} %broadcast.214, s32[3072]{0:T(1024)S(1)} %get-tuple-element.33, f32[3072,4,2]{1,2,0:T(2,128)S(1)} %copy.81), kind=kCustom, calls=%fused_computation.3 | custom fusion | bytes 307200 | tf_op jit(solution)/shard_map/scatter | solution.py:61
  325.9 13.5 %copy.82 = f32[4,2,128,128]{3,2,1,0:T(8,128)S(1)} copy(f32[4,2,128,128]{0,1,3,2:T(2,128)} %bitcast.196) | data formatting | bytes 1048576 | tf_op jit(solution)/shard_map/reshape.18
  339.4 0.6 convolution_bitcast_fusion.3
  340.0 0.6 fusion.5
  340.6 0.6 convolution_bitcast_fusion.2
  341.3 0.6 fusion.3
  341.9 11.4 %copy.122 = f32[1,4,2,128,128]{1,2,4,3,0:T(2,128)} copy(f32[1,4,2,128,128]{4,3,1,2,0:T(8,128)S(1)} %fusion.3) | data formatting | bytes 1048576 | tf_op jit(solution)/shard_map/reshape | solution.py:68
  353.3 27.3 %gather_fusion.2 = f32[3072,4,2]{1,2,0:T(2,128)} fusion(f32[4,2,16384]{0,1,2:T(2,128)} %bitcast.197, s32[3072]{0:T(1024)S(1)} %get-tuple-element.32), kind=kCustom, calls=%fused_computation.2 | custom fusion | bytes 208896 | tf_op jit(solution)/shard_map/gather | solution.py:68
  380.6 2.7 bitcast_bitcast_fusion
  383.2 5.6 reshape.256
  388.8 8.7 %all-to-all-start.1 = ((f32[32,1,768]{2,1,0:T(1,128)}), f32[32,1,768]{2,1,0:T(1,128)S(1)}, u32[]{:S(2)}, u32[]{:S(2)}) async-start(f32[32,1,768]{2,1,0:T(1,128)} %reshape.256), calls=%async_computation.1 | async-start | bytes 196608 | tf_op jit(solution)/shard_map/all_to_all | solution.py:70
  397.5 0.7 add_multiply_fusion
  398.2 8.4 %all-to-all-done.1 = f32[32,1,768]{2,1,0:T(1,128)S(1)} async-done(((f32[32,1,768]{2,1,0:T(1,128)}), f32[32,1,768]{2,1,0:T(1,128)S(1)}, u32[]{:S(2)}, u32[]{:S(2)}) %all-to-all-start.1) | async-done | bytes 98336 | tf_op jit(solution)/shard_map/all_to_all | solution.py:70
  406.6 0.5 broadcast.264
  407.1 0.9 reduce.6
  408.0 4.8 reshape.257
  412.9 4.0 copy.90
  416.9 1.4 fusion.21
  418.3 0.1 stack.104
  418.5 0.3 stack.111
  418.9 5.8 reshape.253
  424.8 15.9 %fusion = f32[3,16,4,3]{1,2,3,0:T(4,128)S(1)} fusion(f32[3,16,24576,1]{2,1,0,3:T(8,128)} %reshape.253, f32[1,3,24576]{2,0,1:T(1,128)S(1)} %copy-done.8, f32[1,1,24576]{2,0,1:T(1,128)S(1)} %bitcast.213, f32[1,1,24576]{2,0,1:T(1,128)S(1)} %bitcast.211, f32[1,1,24576]{2,0,1:T(1,128)S(1)} %bitcast.212, f32[1,3,24576]{2,0,1:T(1,128)S(1)} %stack.111, ...), kind=kOutput, calls=%fused_computation.4 | convolution fusion | flops 171933696 | bytes 5900544 | tf_op jit(solution)/shard_map/il,jl->ij/dot_general | solution.py:84
  440.7 111.1 %psum.7 = f32[3,16,4,3]{1,2,3,0:T(4,128)S(1)} all-reduce(f32[3,16,4,3]{1,2,3,0:T(4,128)S(1)} %fusion), channel_id=1, replica_groups=mesh['band'=16,'ga'=32] {'ga'}, use_global_device_ids=true, to_apply=%region_1.2 | all-reduce | flops 576 | bytes 4608 | tf_op jit(solution)/shard_map/psum | solution.py:87
  551.8 49.0 %all_gather.7 = f32[3,16,4,48]{1,2,3,0:T(4,128)S(1)} all-gather(f32[3,16,4,3]{1,2,3,0:T(4,128)S(1)} %psum.7), channel_id=1, replica_groups=mesh['band'=16,'ga'=32] {'band'}, dimensions={3}, use_global_device_ids=true | all-gather | bytes 39168 | tf_op jit(solution)/shard_map/all_gather | solution.py:88
  600.8 0.2 copy.97
  601.1 0.1 squeeze.17
  601.3 0.1 squeeze.16
  601.5 0.1 maximum_maximum_fusion
  601.6 0.1 copy.102
  601.7 0.1 fusion.68
  601.8 8.8 %cholesky.18 = f32[96,96]{1,0:T(8,128)S(1)} custom-call(f32[96,96]{1,0:T(8,128)S(1)} %fusion.68), custom_call_target="Cholesky" | custom-call | tf_op jit(solution)/shard_map/jit(cholesky)/cholesky | solution.py:93
  610.6 0.6 compare_reduce_fusion
  611.2 0.7 fusion.58
  611.9 7.4 %custom-call.8 = f32[1,96,96]{1,2,0:T(8,128)S(1)} custom-call(f32[1,96,96]{2,1,0:T(8,128)S(1)} %fusion.58), custom_call_target="InvertDiagBlocksLowerTriangular" | custom-call | tf_op jit(solution)/shard_map/jit(_solve_triangular)/triangular_solve | solution.py:95
  619.3 0.1 squeeze.19
  619.4 0.1 squeeze.18
  619.5 0.3 convolution_bitcast_fusion.7
  619.8 0.3 convolution_bitcast_fusion.6
  620.0 0.7 copy.103
  (63 shorter events, 0.6 us)
Async XLA Ops:
  7.2 20.9 %copy-start.19 = (s32[3072]{0:T(1024)S(1)}, s32[3072]{0:T(1024)}, u32[]{:S(2)}) copy-start(s32[3072]{0:T(1024)} %param.16) | copy-start | bytes 36868
  7.2 411.8 %all-gather.2.cloned.1.call-start = ((), (), s32[]{:S(2)}) async-start(), calls=%async_computation.2 | async-start | bytes 5013504 | tf_op jit(solution)/shard_map/all_gather | solution.py:81
  8.0 2.0 copy-start.13
  9.2 24.1 %copy-start.3 = (f32[1,96,256]{2,1,0:T(8,128)}, f32[1,96,256]{2,1,0:T(8,128)S(1)}, u32[]{:S(2)}) copy-start(f32[1,96,256]{2,1,0:T(8,128)S(1)} %get-tuple-element.27) | copy-start | bytes 294916
  9.2 24.1 %copy-start.5 = (f32[1,96,256]{2,1,0:T(8,128)}, f32[1,96,256]{2,1,0:T(8,128)S(1)}, u32[]{:S(2)}) copy-start(f32[1,96,256]{2,1,0:T(8,128)S(1)} %get-tuple-element.30) | copy-start | bytes 294916
  10.0 20.6 %copy-start = (f32[3,1,96,256]{3,2,1,0:T(8,128)S(1)}, f32[3,1,96,256]{3,2,1,0:T(8,128)}, u32[]{:S(2)}) copy-start(f32[3,1,96,256]{3,2,1,0:T(8,128)} %pad_maximum_fusion.4) | copy-start | bytes 884740
  10.3 0.6 copy-start.9
  10.6 18.8 %copy-start.10 = (f32[128,128]{0,1:T(8,128)}, f32[128,128]{0,1:T(8,128)S(1)}, u32[]{:S(2)}) copy-start(f32[128,128]{0,1:T(8,128)S(1)} %get-tuple-element.34) | copy-start | bytes 196612
  10.6 18.8 %copy-start.11 = (f32[128,128]{0,1:T(8,128)}, f32[128,128]{0,1:T(8,128)S(1)}, u32[]{:S(2)}) copy-start(f32[128,128]{0,1:T(8,128)S(1)} %get-tuple-element.35) | copy-start | bytes 196612
  12.1 23.1 %all-to-all-start = ((f32[1,96,2,128]{1,2,0,3:T(2,128)}), f32[1,96,2,128]{1,2,0,3:T(2,128)S(1)}, u32[]{:S(2)}, u32[]{:S(2)}) async-start(f32[1,96,2,128]{1,2,0,3:T(2,128)} %copy.78), calls=%async_computation | async-start | bytes 262144 | tf_op jit(solution)/shard_map/all_to_all | solution.py:57
  325.9 13.5 %copy-start.1 = (f32[1,128,2,128]{1,3,0,2:T(8,128)S(1)}, f32[1,128,2,128]{1,3,0,2:T(8,128)}, u32[]{:S(2)}) copy-start(f32[1,128,2,128]{1,3,0,2:T(8,128)} %get-tuple-element.22) | copy-start | bytes 393220
  325.9 13.5 %copy-start.2 = (f32[1,128,2,128]{1,3,0,2:T(8,128)S(1)}, f32[1,128,2,128]{1,3,0,2:T(8,128)}, u32[]{:S(2)}) copy-start(f32[1,128,2,128]{1,3,0,2:T(8,128)} %get-tuple-element.25) | copy-start | bytes 393220
  325.9 14.1 %copy-start.12 = (f32[4,128,128]{2,1,0:T(8,128)S(1)}, f32[4,128,128]{2,1,0:T(8,128)}, u32[]{:S(2)}) copy-start(f32[4,128,128]{2,1,0:T(8,128)} %param.15) | copy-start | bytes 786436
  388.8 17.8 %all-to-all-start.1 = ((f32[32,1,768]{2,1,0:T(1,128)}), f32[32,1,768]{2,1,0:T(1,128)S(1)}, u32[]{:S(2)}, u32[]{:S(2)}) async-start(f32[32,1,768]{2,1,0:T(1,128)} %reshape.256), calls=%async_computation.1 | async-start | bytes 196608 | tf_op jit(solution)/shard_map/all_to_all | solution.py:70
  408.0 10.4 %copy-start.4 = (f32[1,96,256]{2,1,0:T(8,128)S(1)}, f32[1,96,256]{2,1,0:T(8,128)}, u32[]{:S(2)}) copy-start(f32[1,96,256]{2,1,0:T(8,128)} %copy-done.3) | copy-start | bytes 294916
  408.0 10.4 %copy-start.6 = (f32[1,96,256]{2,1,0:T(8,128)S(1)}, f32[1,96,256]{2,1,0:T(8,128)}, u32[]{:S(2)}) copy-start(f32[1,96,256]{2,1,0:T(8,128)} %copy-done.5) | copy-start | bytes 294916
  418.3 6.4 %copy-start.7 = (f32[1,96,256]{2,1,0:T(8,128)}, f32[1,96,256]{2,1,0:T(8,128)S(1)}, u32[]{:S(2)}) copy-start(f32[1,96,256]{2,1,0:T(8,128)S(1)} %fusion.21) | copy-start | bytes 294916
  418.8 5.9 copy-start.8
  418.9 5.9 copy-start.14
  418.9 5.9 copy-start.15
  418.9 5.9 copy-start.16
  418.9 5.9 copy-start.17
  418.9 5.9 copy-start.18
Sparse Core Ops, SparseCore 0:
  10.2 51.1 all-gather.1
where the time goes:
time: 632 us; the launch traced here: 628 us
  local copies, waits for them, and re-layouts  377 us (60%)
  blocking collectives  160 us (25%)
  other arithmetic  24 us (4%)
  starting transfers between devices  22.4 us (4%)
  matrix products  20.8 us (3%)
  between operations  14.6 us (2%)
  waiting for transfers between devices  9 us (1%)
    scatter x1, local copies, waits for them, and re-layouts, shards(): grid.at[..., stick_column].set(values)  280 us
    psum x1, blocking collectives, shards(): summed = lax.psum(columns, 'ga')  111 us
    all_gather x1, blocking collectives, shards(): whole = lax.all_gather(summed, 'band', axis=3, tiled=True)  49 us
    gather x1, local copies, waits for them, and re-layouts, shards(): grid.reshape(items, planes_dev, 2, count * count)[..., stick_column]  27.3 us
    dot_general x1, matrix products, shards(): product = jnp.einsum('il,jl->ij', flat, own_cols, precision=hi)  15.9 us
    unnamed x44, local copies, waits for them, and re-layouts  14.2 us
    all_to_all x1, starting transfers between devices, shards(): lax.all_to_all(along_x, 'ga', split_axis=3, concat_axis=1, tiled=True)  13.7 us
    another operation x1, local copies, waits for them, and re-layouts  13.5 us
  transfers between devices with their start and end apart: 3, of which 2 were waited for; matrix products, arithmetic and copies ran while one was open for 60% of the time, Pallas kernels for 0%

commit v1 on v0

v1 whole, which is shorter than its diff:
```python
import functools
import math

import jax
import jax.numpy as jnp
import numpy as np
from jax import lax
from jax.experimental import pallas as pl
from jax.experimental.pallas import tpu as pltpu
from jax.sharding import PartitionSpec as P

F32 = jnp.float32
BF16 = jnp.bfloat16
HI = lax.Precision.HIGHEST
ROWS = 8
LANES = 128
NT = (((1,), (1,)), ((), ()))
NN = (((1,), (0,)), ((), ()))
GA_OUT, GA_BACK, SPREAD, TILES, TILE_SUM, TILE_ALL, LATE, LATE_GA, LATE_BAND = range(9)


def dot(a, b, dims=NN, precision=HI):
    return lax.dot_general(a, b, dims, precision=precision, preferred_element_type=F32)


def tables(n, planes):
    half, quarter = n // 2, n // 4
    lane = np.arange(n)
    is_real = (lane < quarter) | (lane >= n - quarter)
    k_of = np.where(is_real, lane, (lane - half) % n)
    fold_k = np.where(k_of < half, k_of, k_of - n)
    groups = n // planes
    x = (np.arange(groups)[:, None, None] * planes + np.arange(planes)[None, None, :]) + np.zeros((1, 2, 1), int)
    part = np.arange(2)[None, :, None] + np.zeros((groups, 1, planes), int)
    x, part = x.reshape(-1), part.reshape(-1)

    def angle(a, b):
        return 2.0 * math.pi * ((a[:, None] * b[None, :]) % n) / n

    th = angle(x, fold_k)
    c, s = np.cos(th), np.sin(th)
    pr = part[:, None] == 0
    ir = is_real[None, :]
    forward = np.where(pr, np.where(ir, c, -s), np.where(ir, s, c))
    inverse = np.where(pr, np.where(ir, c, -s), np.where(ir, s, c)) / float(n) ** 3
    small = np.arange(half)
    small = np.where(small < quarter, small, small - half)
    full = np.arange(n)
    th = angle(small, full)
    c, s = np.cos(th), np.sin(th)
    z_plus = np.concatenate([c, s], axis=1)
    y_plus = np.block([[c.T, -s.T], [s.T, c.T]])
    y_minus = np.block([[c, s], [-s, c]])
    z_real = np.concatenate([c.T, s.T], axis=0)
    z_imag = np.concatenate([-s.T, c.T], axis=0)
    z_minus = np.concatenate([z_real, z_real, z_imag, z_imag], axis=1)
    fx2 = (fold_k.astype(np.float64) ** 2)[None, :]
    return [np.asarray(t, np.float32) for t in (forward, inverse, z_plus, y_plus, y_minus, z_minus, fx2)]


def kernel(n, nb, ng, sd, planes,
           coef_w_in, mask_in, forward_in, hcoef_x_in, hcoef_p_in, coef_x_in, coef_p_in, cols_in, fx2_in,
           z_plus_in, y_plus_in, pot_in, y_minus_in, z_minus_in, inverse_in,
           h_out, red_out,
           coef_w, mask, forward, hcoef_x, hcoef_p, coef_x, coef_p, cols, fx2,
           z_plus, y_plus, pot, y_minus, z_minus, inverse,
           src, ga_src, ga_in, hot, back_src, back_in, spread, own, ss2, early, tiles, tile_sum, tile_in,
           tile_all, hw, late, late_part, late_in, late_sum, late_all, big_a, big_b, kin_ref, gauge, q_cols, send, recv, load):
    half, quarter = n // 2, n // 4
    rb = 2 * planes
    sp = hot.shape[2]
    cells = rb * half
    nslice = sd // ROWS
    width = 3 * nb
    ntile = 5 * nb // ROWS
    b = lax.axis_index("band")
    g = lax.axis_index("ga")
    lane = lax.broadcasted_iota(jnp.int32, (1, n), 1)
    real_lane = (lane < quarter) | (lane >= n - quarter)
    sign = jnp.where(real_lane, -1.0, 1.0).astype(F32)

    def swap(v):
        return pltpu.roll(v, half, 1)

    def pack(ref):
        v = ref[0]
        return jnp.where(real_lane, v[:, :n], swap(v[:, n:]))

    def rows(i, count=ROWS):
        return pl.ds(pl.multiple_of(i * count, count), count)

    def each(count, me, body):
        def step(d, carry):
            body(lax.rem(me + d, count))
            return carry
        lax.fori_loop(1, count, step, 0)

    def push(src_ref, dst_ref, phase, where):
        pltpu.make_async_remote_copy(
            src_ref=src_ref, dst_ref=dst_ref, send_sem=send.at[phase], recv_sem=recv.at[phase],
            device_id=where, device_id_type=pl.DeviceIdType.MESH).start()

    def wait_rows(ref, count, sem):
        piece = ref.at[pl.ds(0, count)]
        pltpu.make_async_copy(piece, piece, sem).wait()

    def wait_from(ref, sources, size, sem):
        if sources >= nb:
            wait_rows(ref, (nb - 1) * size, sem)
        else:
            @pl.when(b < sources)
            def _():
                wait_rows(ref, (sources - 1) * size, sem)

            @pl.when(b >= sources)
            def _():
                wait_rows(ref, sources * size, sem)

    held = [coef_w, mask, forward, hcoef_x, hcoef_p, coef_x, coef_p, cols, fx2,
            z_plus, y_plus, pot, y_minus, z_minus, inverse]
    given = [coef_w_in, mask_in, forward_in, hcoef_x_in, hcoef_p_in, coef_x_in, coef_p_in, cols_in, fx2_in,
             z_plus_in, y_plus_in, pot_in, y_minus_in, z_minus_in, inverse_in]
    loads = [pltpu.make_async_copy(a, v, load.at[i]) for i, (a, v) in enumerate(zip(given, held))]
    for copy in loads:
        copy.start()

    barrier = pltpu.get_barrier_semaphore()

    def greet_ga(p):
        pl.semaphore_signal(barrier, inc=1, device_id=(b, p), device_id_type=pl.DeviceIdType.MESH)

    def greet_band(p):
        pl.semaphore_signal(barrier, inc=1, device_id=(p, g), device_id_type=pl.DeviceIdType.MESH)

    each(ng, g, greet_ga)
    each(nb, b, greet_band)

    for copy in loads[:3]:
        copy.wait()
    m = mask[...].astype(F32)
    pm = jnp.where(real_lane, m, swap(m))
    w = pack(coef_w) * pm
    src[3] = w
    wide = jnp.concatenate([w, jnp.zeros((sp - sd, n), F32)], axis=0) if sp > sd else w
    ga_src[...] = dot(forward[...], wide, NT)
    for copy in loads[3:7]:
        copy.wait()
    src[0] = pack(hcoef_x) * pm
    src[1] = pack(hcoef_p) * pm
    src[2] = pack(coef_x) * pm
    src[4] = pack(coef_p) * pm

    pl.semaphore_wait(barrier, ng + nb - 2)

    def send_ga(p):
        push(ga_src.at[rows(p, rb)], ga_in.at[rows(g, rb)], GA_OUT, (b, p))

    each(ng, g, send_ga)
    ga_in[rows(g, rb), :] = ga_src[rows(g, rb), :]

    def send_spread(p):
        @pl.when(p < nslice)
        def _():
            push(src.at[:, rows(p), :], spread.at[:, rows(b), :], SPREAD, (p, g))

    each(nb, b, send_spread)

    @pl.when(b < nslice)
    def _():
        spread[:, rows(b), :] = src[:, rows(b), :]

    for copy in loads[7:9]:
        copy.wait()

    fourth = n // 4
    strided = [cols[pl.ds(t, ng // 4, stride=3), :] for t in range(3)]
    lane32 = lax.broadcasted_iota(jnp.int32, (1, n), 1)
    q_cols[0] = strided[0]
    q_cols[1] = jnp.where(lane32 < fourth, pltpu.roll(strided[0], fourth, 1), pltpu.roll(strided[1], fourth, 1))
    q_cols[2] = jnp.where(lane32 < half, pltpu.roll(strided[1], half, 1), pltpu.roll(strided[2], half, 1))
    q_cols[3] = pltpu.roll(strided[2], 3 * fourth, 1)

    def cols_of(q):
        return q_cols[lax.rem(q, 4), pl.ds(q // 4, 1), :]

    def make_hot(q, carry):
        zc = cols_of(q) & (half - 1)
        one = jnp.where(lax.broadcasted_iota(jnp.int32, (half, sp), 0) == zc, 1.0, 0.0).astype(BF16)
        hot[q] = jnp.concatenate([one, one], axis=0)
        return carry

    lax.fori_loop(0, ng, make_hot, 0)

    def folded(v):
        return jnp.where(v < half, v, v - n)

    mine = cols_of(g)
    fy, fz = folded(mine // n), folded(mine & (n - 1))
    radial = jnp.broadcast_to((fy * fy + fz * fz).astype(F32), (n, sp)).T[:sd]
    kin_ref[...] = 0.5 * (2.0 * math.pi / n) ** 2 * (fx2[...] + radial)

    wait_rows(ga_in, (ng - 1) * rb, recv.at[GA_OUT])

    def y_hot(q):
        yc = (cols_of(q) // n) & (half - 1)
        return lax.broadcasted_iota(jnp.int32, (half, sp), 0) == yc

    group = 4 if ng % 4 == 0 else 2

    def scatter(i, acc):
        left, right = [], []
        for t in range(group):
            q = i * group + t
            v = ga_in[rows(q, rb), :]
            high = v.astype(BF16).astype(F32)
            low = v - high
            here = y_hot(q)[None]
            one = hot[q][:half]
            for piece in (high, low):
                spreadout = jnp.where(here, piece[:, None, :], 0.0).reshape(cells, sp)
                left.append(spreadout.astype(BF16))
                right.append(one)
        return acc + dot(jnp.concatenate(left, axis=1), jnp.concatenate(right, axis=1), NT, None)

    grid = lax.fori_loop(0, ng // group, scatter, jnp.zeros((cells, half), F32))

    for copy in loads[9:]:
        copy.wait()
    mid = planes * half
    turned = dot(grid, z_plus[...])
    f_re = turned[:mid, :n] - turned[mid:, n:]
    f_im = turned[:mid, n:] + turned[mid:, :n]
    stacked = jnp.concatenate(
        [jnp.concatenate([f_re[j * half:(j + 1) * half], f_im[j * half:(j + 1) * half]], axis=0)
         for j in range(planes)], axis=1)
    field = dot(y_plus[...], stacked)
    potential = jnp.concatenate([pot[j] for j in range(planes)], axis=1)
    product = jnp.concatenate([field[:n] * potential, field[n:] * potential], axis=0)
    product = dot(y_minus[...], product)
    product = jnp.concatenate(
        [jnp.concatenate([product[:half, j * n:(j + 1) * n], product[half:, j * n:(j + 1) * n]], axis=1)
         for j in range(planes)], axis=0)
    product = dot(product, z_minus[...])
    product = jnp.concatenate([product[:, :n], product[:, n:]], axis=0)
    high = product.astype(BF16).astype(F32)
    low = product - high
    both = jnp.where(lax.broadcasted_iota(jnp.int32, (1, n), 1) < half, high, low).astype(BF16)

    def gather(i, carry):
        pair = jnp.concatenate([hot[2 * i], hot[2 * i + 1]], axis=1)
        found = dot(both, pair, NN, None)
        for t in range(2):
            q = 2 * i + t
            here = y_hot(q)[None]
            part = found[:, t * sp:(t + 1) * sp].reshape(rb, half, sp)
            back_src[rows(q, rb), :] = jnp.sum(jnp.where(here, part, 0.0), axis=1)

            @pl.when(q != g)
            def _():
                push(back_src.at[rows(q, rb)], back_in.at[rows(g, rb)], GA_BACK, (b, q))
        return carry

    lax.fori_loop(0, ng // 2, gather, 0)
    back_in[rows(g, rb), :] = back_src[rows(g, rb), :]

    @pl.when(b < nslice)
    def _():
        piece = spread.at[0:5, pl.ds(0, (nb - 1) * ROWS)]
        pltpu.make_async_copy(piece, piece, recv.at[SPREAD]).wait()
        left, right = [], []
        for r in range(ROWS):
            vec = [spread[a, pl.ds(r, nb, stride=ROWS), :] for a in range(5)]
            s = jnp.concatenate(vec[2:], axis=0)
            left.append(jnp.concatenate(vec, axis=0))
            right.append(jnp.concatenate([s, swap(s) * sign], axis=0))
        right = jnp.concatenate(right, axis=1)
        ss2[...] = right
        early[:, :2 * width] = dot(jnp.concatenate(left, axis=1), right, NT)

        def send_tile(p):
            @pl.when(p < ntile)
            def _():
                push(early.at[rows(p)], tiles.at[rows(b)], TILES, (p, g))

        each(nb, b, send_tile)

        @pl.when(b < ntile)
        def _():
            tiles[rows(b), :] = early[rows(b), :]

    wait_rows(back_in, (ng - 1) * rb, recv.at[GA_BACK])
    local = dot(back_in[...].T, inverse[...])[:sd]
    h = pm * (kin_ref[...] * w + local)
    hw[...] = h

    def send_late(p):
        @pl.when(p < nslice)
        def _():
            push(hw.at[rows(p)], late.at[rows(b)], LATE, (p, g))

    each(nb, b, send_late)

    @pl.when(b < nslice)
    def _():
        late[rows(b), :] = hw[rows(b), :]

    h_out[0, :, :n] = jnp.where(real_lane, h, 0.0)
    h_out[0, :, n:] = jnp.where(real_lane, swap(h), 0.0)

    @pl.when(b < ntile)
    def _():
        wait_from(tiles, nslice, ROWS, recv.at[TILES])
        tile_sum[...] = jnp.sum(tiles[:nslice * ROWS, :].reshape(nslice, ROWS, LANES), axis=0)

        def send_sum(p):
            push(tile_sum, tile_in.at[rows(g)], TILE_SUM, (b, p))

        each(ng, g, send_sum)
        tile_in[rows(g), :] = tile_sum[...]

    @pl.when(b < nslice)
    def _():
        wait_rows(late, (nb - 1) * ROWS, recv.at[LATE])
        left = jnp.concatenate([late[pl.ds(r, nb, stride=ROWS), :] for r in range(ROWS)], axis=1)
        late_part[:, :2 * width] = dot(left, ss2[...], NT)

        def send_part(p):
            push(late_part, late_in.at[rows(g, nb)], LATE_GA, (b, p))

        each(ng, g, send_part)
        late_in[rows(g, nb), :] = late_part[...]

    @pl.when(b < ntile)
    def _():
        wait_rows(tile_in, (ng - 1) * ROWS, recv.at[TILE_SUM])
        tile_all[rows(b), :] = jnp.sum(tile_in[...].reshape(ng, ROWS, LANES), axis=0)

        def send_all(p):
            push(tile_all.at[rows(b)], tile_all.at[rows(b)], TILE_ALL, (p, g))

        each(nb, b, send_all)

    @pl.when(b < nslice)
    def _():
        wait_rows(late_in, (ng - 1) * nb, recv.at[LATE_GA])
        late_all[rows(b, nb), :] = jnp.sum(late_in[:ng * nb, :].reshape(ng, nb, LANES), axis=0)

        def send_whole(p):
            push(late_all.at[rows(b, nb)], late_all.at[rows(b, nb)], LATE_BAND, (p, g))

        each(nb, b, send_whole)

    wait_from(tile_all, ntile, ROWS, recv.at[TILE_ALL])

    def full(top):
        return jnp.concatenate(
            [top, jnp.concatenate([-top[:, width:2 * width], top[:, :width]], axis=1)], axis=0)

    size = 2 * width
    big_a[...] = full(tile_all[2 * nb:, :size])
    here = lax.broadcasted_iota(jnp.int32, (size, size), 0)
    there = lax.broadcasted_iota(jnp.int32, (size, size), 1)
    big_b[...] = jnp.where(here == there, 1.0, 0.0).astype(F32)
    row_id = lax.broadcasted_iota(jnp.int32, (size, 1), 0)
    col_id = lax.broadcasted_iota(jnp.int32, (1, size), 1)

    def eliminate(j, carry):
        a, inv = big_a[...], big_b[...]
        row, inv_row = big_a[pl.ds(j, 1), :], big_b[pl.ds(j, 1), :]
        pivot = jnp.sum(jnp.where(col_id == j, row, 0.0), axis=1, keepdims=True)
        column = jnp.sum(jnp.where(col_id == j, a, 0.0), axis=1, keepdims=True)
        column = jnp.where(row_id > j, column, 0.0)
        scale = 1.0 / pivot
        big_a[...] = a - column * (row * scale)
        big_b[...] = inv - column * (inv_row * scale)
        return carry

    lax.fori_loop(0, size, eliminate, 0)
    diag = jnp.sum(jnp.where(here == there, big_a[...], 0.0), axis=1, keepdims=True)
    lower_inv = big_b[...] / jnp.sqrt(diag)

    wait_from(late_all, nslice, nb, recv.at[LATE_BAND])
    late_gram = jnp.sum(late_all[:nslice * nb, :].reshape(nslice, nb, LANES), axis=0)
    top = jnp.concatenate([tile_all[:nb, :size], late_gram[:, :size], tile_all[nb:2 * nb, :size]], axis=0)
    red_out[...] = dot(dot(lower_inv, full(top), NT), lower_inv, NT)

    wait_rows(gauge, (ng - 1) * rb, send.at[GA_OUT])
    wait_rows(gauge, (ng - 1) * rb, send.at[GA_BACK])
    wait_from(gauge, nslice, 5 * ROWS, send.at[SPREAD])
    wait_from(gauge, nslice, ROWS, send.at[LATE])

    @pl.when(b < nslice)
    def _():
        wait_from(late_in, ntile, ROWS, send.at[TILES])
        wait_rows(late_in, (ng - 1) * nb, send.at[LATE_GA])
        wait_rows(late_in, (nb - 1) * nb, send.at[LATE_BAND])

    @pl.when(b < ntile)
    def _():
        wait_rows(late_in, (ng - 1) * ROWS, send.at[TILE_SUM])
        wait_rows(late_in, (nb - 1) * ROWS, send.at[TILE_ALL])


def solution(mesh):
    nb, ng = mesh.shape["band"], mesh.shape["ga"]

    def shards(coef_x, coef_w, coef_p, hcoef_x, hcoef_p, potential, stick_column, sphere_mask):
        n = potential.shape[1]
        planes = potential.shape[0]
        sd = sphere_mask.shape[0]
        sp = n
        rb = 2 * planes
        half = n // 2
        cols = stick_column.reshape(ng * sd // n, n)
        size = 6 * nb
        ntile = 5 * nb // ROWS
        vmem = lambda *shape: pltpu.VMEM(shape, F32)
        scratch = [
            vmem(5, sd, n), vmem(2 * n, sp), vmem(2 * n, sp), pltpu.VMEM((ng, 2 * half, sp), BF16),
            vmem(2 * n, sp), vmem(2 * n, sp), vmem(5, nb * ROWS, n), vmem(ROWS, n),
            vmem(size, ROWS * n), vmem(5 * nb, LANES), vmem(nb * ROWS, LANES), vmem(ROWS, LANES),
            vmem(ng * ROWS, LANES), vmem(5 * nb, LANES), vmem(sd, n), vmem(nb * ROWS, n), vmem(nb, LANES),
            vmem(max(ng, nb) * nb, LANES), vmem(nb, LANES), vmem(nb * nb, LANES), vmem(size, size), vmem(size, size), vmem(sd, n),
            vmem(max(ng * rb, 5 * sd, nb * ROWS), n), pltpu.VMEM((4, ng // 4, n), jnp.int32),
            pltpu.SemaphoreType.DMA((9,)), pltpu.SemaphoreType.DMA((9,)), pltpu.SemaphoreType.DMA((15,)),
        ]
        forward, inverse, z_plus, y_plus, y_minus, z_minus, fx2 = [jnp.asarray(t) for t in tables(n, planes)]
        args = [coef_w, sphere_mask, forward, hcoef_x, hcoef_p, coef_x, coef_p, cols, fx2,
                z_plus, y_plus, potential, y_minus, z_minus, inverse]
        scratch = [pltpu.VMEM(a.shape, a.dtype) for a in args] + scratch
        return pl.pallas_call(
            functools.partial(kernel, n, nb, ng, sd, planes),
            out_shape=[jax.ShapeDtypeStruct(coef_w.shape, F32), jax.ShapeDtypeStruct((size, size), F32)],
            in_specs=[pl.BlockSpec(memory_space=pltpu.HBM)] * len(args),
            out_specs=[pl.BlockSpec(memory_space=pltpu.VMEM)] * 2,
            scratch_shapes=scratch,
            compiler_params=pltpu.CompilerParams(
                collective_id=0, has_side_effects=True, vmem_limit_bytes=60 * 1024 * 1024),
        )(*args)

    vec = P("band", "ga", None)
    in_specs = (vec, vec, vec, vec, vec, P("ga", None, None), P(), P("ga", None))
    return jax.shard_map(shards, mesh=mesh, in_specs=in_specs, out_specs=(vec, P()), check_vma=False)
```

time: 632 us -> 66.5 us (0.11)
  local copies, waits for them, and re-layouts: 377 us -> 2.18 us
  blocking collectives: 160 us -> 0 us
  Pallas kernels: 0 us -> 63.5 us
  other arithmetic: 24 us -> 0 us
  starting transfers between devices: 22.4 us -> 0 us
  matrix products: 20.8 us -> 0 us
  between operations: 14.6 us -> 0.65 us
  waiting for transfers between devices: 9 us -> 0 us
    scatter x1 -> x0, local copies, waits for them, and re-layouts: 280 us -> none  [shards(): grid.at[..., stick_column].set(values)]
    psum x1 -> x0, blocking collectives: 111 us -> none  [shards(): summed = lax.psum(columns, 'ga')]
    pallas_call x0 -> x1, Pallas kernels: none -> 63.5 us  [shards(): pl.pallas_call(functools.partial(kernel, n, nb, ng, sd, planes), out_shap...]
    all_gather x1 -> x0, blocking collectives: 49 us -> none  [shards(): whole = lax.all_gather(summed, 'band', axis=3, tiled=True)]
    gather x3 -> x0, local copies, waits for them, and re-layouts: 29.7 us -> none  [the longest x1 27.3 us: shards(): grid.reshape(items, planes_dev, 2, count * count)[..., stick_column]]
    all_to_all x2 -> x0, starting transfers between devices: 22.4 us -> none  [the longest x1 13.7 us: shards(): lax.all_to_all(along_x, 'ga', split_axis=3, concat_axis=1, tiled=True)]
    dot_general x7 -> x0, matrix products: 20.2 us -> none  [the longest x1 15.9 us: shards(): product = jnp.einsum('il,jl->ij', flat, own_cols, precision=hi)]
    another operation x8 -> x0, other arithmetic: 19.1 us -> none  [the longest x3 9.45 us: shards(): lower = jnp.linalg.cholesky(big_s)]
  transfers between devices with their start and end apart: 3 -> 0, of which waited for: 2 -> 0; matrix products, arithmetic and copies ran while one was open for 60% -> 0% of each run, Pallas kernels for 0% -> 0%
where the time goes in v1:
time: 66.5 us; the launch traced here: 66.3 us
  Pallas kernels  63.5 us (95%)
  local copies, waits for them, and re-layouts  2.18 us (3%)
    pallas_call x1, Pallas kernels, shards(): pl.pallas_call(functools.partial(kernel, n, nb, ng, sd, planes), out_shap...  63.5 us
    unnamed x4, local copies, waits for them, and re-layouts  2.18 us

profile of v1, /device:TPU:1, one launch (start us, length us, event | category | flops | bytes accessed | tf_op | source)
XLA Modules:
  0.0 66.3 jit_solution(7832637409287094935)
XLA Ops:
  0.6 63.5 %shard_map.158 = (f32[1,96,256]{2,1,0:T(8,128)}, f32[96,96]{1,0:T(8,128)}) custom-call(f32[1,96,256]{2,1,0:T(8,128)} %coef_w_in.1, s32[96,128]{1,0:T(8,128)} %mask_in.1, f32[256,128]{1,0:T(8,128)} %constant.14.clone.forward_in, f32[1,96,256]{2,1,0:T(8,128)} %hcoef_x_in.1, f32[1,96,256]{2,1,0:T(8,128)} %hcoef_p_in.1, f32[1,96,256]{2,1,0:T(8,128)} %coef_x_in.1, ...), custom_call_target="tpu_custom_call" | custom-call | tf_op jit(solution)/shard_map/pallas_call | solution.py:431
  64.1 0.0 copy-start
  64.1 1.6 %copy.19 = f32[1,96,256]{2,1,0:T(8,128)} copy(f32[1,96,256]{2,1,0:T(8,128)} %get-tuple-element.4) | data formatting | bytes 196608
  65.7 0.0 copy-done
  65.7 0.6 copy.20
Async XLA Ops:
  64.1 1.6 %copy-start = (f32[96,96]{1,0:T(8,128)S(1)}, f32[96,96]{1,0:T(8,128)}, u32[]{:S(2)}) copy-start(f32[96,96]{1,0:T(8,128)} %get-tuple-element.5) | copy-start | bytes 110596

commit v2 on v1

v2 whole, which is shorter than its diff:
```python
import functools
import math

import jax
import jax.numpy as jnp
import ml_dtypes
import numpy as np
from jax import lax
from jax.experimental import pallas as pl
from jax.experimental.pallas import tpu as pltpu
from jax.sharding import PartitionSpec as P

F32 = jnp.float32
BF16 = jnp.bfloat16
HI = lax.Precision.HIGHEST
ROWS = 8
LANES = 128
NT = (((1,), (1,)), ((), ()))
NN = (((1,), (0,)), ((), ()))
GA_OUT, GA_BACK, GROUP, MATES, EARLY, EARLY_GA, EARLY_BAND, LATE, LATE_GA, LATE_BAND = range(10)
TEAM = 4


def dot(a, b, dims=NN, precision=HI):
    return lax.dot_general(a, b, dims, precision=precision, preferred_element_type=F32)


def tables(n, planes):
    half, quarter = n // 2, n // 4
    lane = np.arange(n)
    is_real = (lane < quarter) | (lane >= n - quarter)
    k_of = np.where(is_real, lane, (lane - half) % n)
    fold_k = np.where(k_of < half, k_of, k_of - n)
    groups = n // planes
    x = (np.arange(groups)[:, None, None] * planes + np.arange(planes)[None, None, :]) + np.zeros((1, 2, 1), int)
    part = np.arange(2)[None, :, None] + np.zeros((groups, 1, planes), int)
    x, part = x.reshape(-1), part.reshape(-1)

    def angle(a, b):
        return 2.0 * math.pi * ((a[:, None] * b[None, :]) % n) / n

    th = angle(x, fold_k)
    c, s = np.cos(th), np.sin(th)
    pr = part[:, None] == 0
    ir = is_real[None, :]
    forward = np.where(pr, np.where(ir, c, -s), np.where(ir, s, c))
    inverse = np.where(pr, np.where(ir, c, -s), np.where(ir, s, c)) / float(n) ** 3
    small = np.arange(half)
    small = np.where(small < quarter, small, small - half)
    full = np.arange(n)
    th = angle(small, full)
    c, s = np.cos(th), np.sin(th)
    z_plus = np.concatenate([c, s], axis=1)
    y_plus = np.block([[c.T, -s.T], [s.T, c.T]])
    y_minus = np.block([[c, s], [-s, c]])
    z_real = np.concatenate([c.T, s.T], axis=0)
    z_imag = np.concatenate([-s.T, c.T], axis=0)
    z_minus = np.concatenate([z_real, z_real, z_imag, z_imag], axis=1)
    fx2 = (fold_k.astype(np.float64) ** 2)[None, :]
    pairs = []
    for t in (forward, inverse, z_plus, y_plus, y_minus, z_minus):
        high = t.astype(ml_dtypes.bfloat16)
        pairs.append(np.stack([high, (t - high.astype(np.float64)).astype(ml_dtypes.bfloat16)]))
    return pairs + [fx2.astype(np.float32)]


def kernel(n, nb, ng, sd, planes,
           coef_w_in, mask_in, forward_in, hcoef_x_in, hcoef_p_in, coef_x_in, coef_p_in, cols_in, fx2_in,
           z_plus_in, y_plus_in, pot_in, y_minus_in, z_minus_in, inverse_in,
           h_out, red_out,
           coef_w, mask, forward, hcoef_x, hcoef_p, coef_x, coef_p, cols, fx2,
           z_plus, y_plus, pot, y_minus, z_minus, inverse,
           src, ga_src, ga_in, hot, back_src, back_in, share, rows_src, ss_high, ss_low, early, early_in,
           early_mine, early_ga, early_all, hw, late, late_part, late_in, late_all, big_a, big_b, kin_ref, q_cols, send, recv, load):
    half, quarter = n // 2, n // 4
    rb = 2 * planes
    sp = hot.shape[2]
    cells = rb * half
    width = 3 * nb
    size = 2 * width
    part = sd // TEAM
    b = lax.axis_index("band")
    g = lax.axis_index("ga")
    seat = lax.rem(b, TEAM)
    team = b - seat
    lane = lax.broadcasted_iota(jnp.int32, (1, n), 1)
    real_lane = (lane < quarter) | (lane >= n - quarter)
    sign = jnp.where(real_lane, -1.0, 1.0).astype(F32)

    def swap(v):
        return pltpu.roll(v, half, 1)

    def pack(ref):
        v = ref[0]
        return jnp.where(real_lane, v[:, :n], swap(v[:, n:]))

    def rows(i, count=ROWS):
        return pl.ds(pl.multiple_of(i * count, count), count)

    def each(count, me, body):
        def step(k, carry):
            d = count // 2 + (k + 1) // 2 * (2 * lax.rem(k, 2) - 1)
            body(lax.rem(me + d, count))
            return carry
        lax.fori_loop(0, count - 1, step, 0)

    def push(src_ref, dst_ref, phase, where):
        pltpu.make_async_remote_copy(
            src_ref=src_ref, dst_ref=dst_ref, send_sem=send.at[phase], recv_sem=recv.at[phase],
            device_id=where, device_id_type=pl.DeviceIdType.MESH).start()

    def wait_for(piece, sem):
        pltpu.make_async_copy(piece, piece, sem).wait()

    def wait_rows(ref, count, sem):
        wait_for(ref.at[pl.ds(0, count)], sem)

    def split(v):
        high = v.astype(BF16)
        return high, (v - high.astype(F32)).astype(BF16)

    def dot3(a, b, dims=NN):
        return dot(a[0], b[0], dims, None) + (dot(a[0], b[1], dims, None) + dot(a[1], b[0], dims, None))

    def pair(table):
        return table[0], table[1]

    def gram(left, s_high, s_low):
        count = left.shape[0]
        high, low = split(left)
        upper = dot(jnp.concatenate([high, low], axis=0), s_high, NT, None)
        return upper[:count] + upper[count:] + dot(high, s_low, NT, None)

    held = [coef_w, mask, forward, hcoef_x, hcoef_p, coef_x, coef_p, cols, fx2,
            z_plus, y_plus, pot, y_minus, z_minus, inverse]
    given = [coef_w_in, mask_in, forward_in, hcoef_x_in, hcoef_p_in, coef_x_in, coef_p_in, cols_in, fx2_in,
             z_plus_in, y_plus_in, pot_in, y_minus_in, z_minus_in, inverse_in]
    loads = [pltpu.make_async_copy(a, v, load.at[i]) for i, (a, v) in enumerate(zip(given, held))]
    for copy in loads[:3]:
        copy.start()

    barrier = pltpu.get_barrier_semaphore()

    def greet_ga(p):
        pl.semaphore_signal(barrier, inc=1, device_id=(b, p), device_id_type=pl.DeviceIdType.MESH)

    def greet_band(p):
        pl.semaphore_signal(barrier, inc=1, device_id=(p, g), device_id_type=pl.DeviceIdType.MESH)

    each(ng, g, greet_ga)
    each(nb, b, greet_band)
    for copy in loads[3:]:
        copy.start()

    for copy in loads[:3]:
        copy.wait()
    m = mask[...].astype(F32)
    pm = jnp.where(real_lane, m, swap(m))
    w = pack(coef_w) * pm
    src[3] = w
    wide = jnp.concatenate([w, jnp.zeros((sp - sd, n), F32)], axis=0) if sp > sd else w
    ga_src[...] = dot3(pair(forward), split(wide), NT)
    pl.semaphore_wait(barrier, ng + nb - 2)

    def send_ga(p):
        push(ga_src.at[rows(p, rb)], ga_in.at[rows(g, rb)], GA_OUT, (b, p))

    each(ng, g, send_ga)
    ga_in[rows(g, rb), :] = ga_src[rows(g, rb), :]

    for copy in loads[3:7]:
        copy.wait()
    src[0] = pack(hcoef_x) * pm
    src[1] = pack(hcoef_p) * pm
    src[2] = pack(coef_x) * pm
    src[4] = pack(coef_p) * pm

    def seat_rows(p):
        return pl.ds(pl.multiple_of(p * part, ROWS), part)

    def send_group(p):
        push(src.at[pl.ds(2, 3), seat_rows(lax.rem(p, TEAM))], share.at[:, seat_rows(b)], GROUP, (p, g))

    each(nb, b, send_group)
    share[:, seat_rows(b), :] = src[2:5, seat_rows(seat), :]

    def each_mate(body):
        def step(d, carry):
            body(lax.rem(seat + d, TEAM))
            return carry
        lax.fori_loop(1, TEAM, step, 0)

    def send_mate(other):
        for a in range(2):
            push(src.at[a, seat_rows(other)], rows_src.at[seat_rows(a * TEAM + seat)], MATES, (team + other, g))

    each_mate(send_mate)
    for a in range(2):
        rows_src[seat_rows(a * TEAM + seat), :] = src[a, seat_rows(seat), :]

    for copy in loads[7:9]:
        copy.wait()

    fourth = n // 4
    strided = [cols[pl.ds(t, ng // 4, stride=3), :] for t in range(3)]
    lane32 = lax.broadcasted_iota(jnp.int32, (1, n), 1)
    q_cols[0] = strided[0]
    q_cols[1] = jnp.where(lane32 < fourth, pltpu.roll(strided[0], fourth, 1), pltpu.roll(strided[1], fourth, 1))
    q_cols[2] = jnp.where(lane32 < half, pltpu.roll(strided[1], half, 1), pltpu.roll(strided[2], half, 1))
    q_cols[3] = pltpu.roll(strided[2], 3 * fourth, 1)

    def cols_of(q):
        return q_cols[lax.rem(q, 4), pl.ds(q // 4, 1), :]

    def make_hot(q, carry):
        zc = cols_of(q) & (half - 1)
        one = jnp.where(lax.broadcasted_iota(jnp.int32, (half, sp), 0) == zc, 1.0, 0.0).astype(BF16)
        hot[q] = jnp.concatenate([one, one], axis=0)
        return carry

    lax.fori_loop(0, ng, make_hot, 0)

    def folded(v):
        return jnp.where(v < half, v, v - n)

    mine = cols_of(g)
    fy, fz = folded(mine // n), folded(mine & (n - 1))
    radial = jnp.broadcast_to((fy * fy + fz * fz).astype(F32), (n, sp)).T[:sd]
    kin_ref[...] = 0.5 * (2.0 * math.pi / n) ** 2 * (fx2[...] + radial)

    wait_rows(ga_in, (ng - 1) * rb, recv.at[GA_OUT])

    def y_hot(q):
        yc = (cols_of(q) // n) & (half - 1)
        return lax.broadcasted_iota(jnp.int32, (half, sp), 0) == yc

    group = 4 if ng % 4 == 0 else 2

    def scatter(i, acc):
        left, right = [], []
        for t in range(group):
            q = i * group + t
            v = ga_in[rows(q, rb), :]
            high = v.astype(BF16).astype(F32)
            low = v - high
            here = y_hot(q)[None]
            one = hot[q][:half]
            for piece in (high, low):
                spreadout = jnp.where(here, piece[:, None, :], 0.0).reshape(cells, sp)
                left.append(spreadout.astype(BF16))
                right.append(one)
        return acc + dot(jnp.concatenate(left, axis=1), jnp.concatenate(right, axis=1), NT, None)

    grid = lax.fori_loop(0, ng // group, scatter, jnp.zeros((cells, half), F32))

    for copy in loads[9:]:
        copy.wait()
    mid = planes * half
    turned = dot3(split(grid), pair(z_plus))
    f_re = turned[:mid, :n] - turned[mid:, n:]
    f_im = turned[:mid, n:] + turned[mid:, :n]
    stacked = jnp.concatenate(
        [jnp.concatenate([f_re[j * half:(j + 1) * half], f_im[j * half:(j + 1) * half]], axis=0)
         for j in range(planes)], axis=1)
    field = dot3(pair(y_plus), split(stacked))
    potential = jnp.concatenate([pot[j] for j in range(planes)], axis=1)
    product = jnp.concatenate([field[:n] * potential, field[n:] * potential], axis=0)
    product = dot3(pair(y_minus), split(product))
    product = jnp.concatenate(
        [jnp.concatenate([product[:half, j * n:(j + 1) * n], product[half:, j * n:(j + 1) * n]], axis=1)
         for j in range(planes)], axis=0)
    product = dot3(split(product), pair(z_minus))
    product = jnp.concatenate([product[:, :n], product[:, n:]], axis=0)
    high = product.astype(BF16).astype(F32)
    low = product - high
    both = jnp.where(lax.broadcasted_iota(jnp.int32, (1, n), 1) < half, high, low).astype(BF16)

    def gather(i, carry):
        pair = jnp.concatenate([hot[2 * i], hot[2 * i + 1]], axis=1)
        found = dot(both, pair, NN, None)
        for t in range(2):
            q = 2 * i + t
            here = y_hot(q)[None]
            part = found[:, t * sp:(t + 1) * sp].reshape(rb, half, sp)
            back_src[rows(q, rb), :] = jnp.sum(jnp.where(here, part, 0.0), axis=1)

            @pl.when(q != g)
            def _():
                push(back_src.at[rows(q, rb)], back_in.at[rows(g, rb)], GA_BACK, (b, q))
        return carry

    lax.fori_loop(0, ng // 2, gather, 0)
    back_in[rows(g, rb), :] = back_src[rows(g, rb), :]

    wait_for(share.at[:, pl.ds(0, (nb - 1) * part)], recv.at[GROUP])

    def make_span(i, carry):
        for t in range(3):
            r = i * 3 + t
            s = jnp.concatenate([share[a, pl.ds(r, nb, stride=part), :] for a in range(3)], axis=0)
            high, low = split(jnp.concatenate([s, swap(s) * sign], axis=0))
            at = pl.ds(pl.multiple_of(r * n, n), n)
            ss_high[:, at] = high
            ss_low[:, at] = low
        return carry

    lax.fori_loop(0, part // 3, make_span, 0)
    wait_rows(rows_src, 2 * (TEAM - 1) * part, recv.at[MATES])
    for a in range(3):
        rows_src[(2 + a) * TEAM * part:(3 + a) * TEAM * part] = share[a, pl.ds(pl.multiple_of(team * part, ROWS), TEAM * part), :]
    found = gram(jnp.concatenate([rows_src[pl.ds(r, 5 * TEAM, stride=part), :] for r in range(part)], axis=1),
                 ss_high[...], ss_low[...])
    for t in range(TEAM):
        for a in range(5):
            early[t, a, :, :size] = found[a * TEAM + t:a * TEAM + t + 1]

    def send_early(other):
        push(early.at[other], early_in.at[seat], EARLY, (team + other, g))

    each_mate(send_early)
    early_in[seat] = early[seat]
    wait_rows(early_in, TEAM - 1, recv.at[EARLY])
    early_mine[...] = jnp.sum(early_in[...], axis=0)

    def send_mine(p):
        push(early_mine, early_ga.at[g], EARLY_GA, (b, p))

    each(ng, g, send_mine)
    early_ga[g] = early_mine[...]
    wait_rows(back_in, (ng - 1) * rb, recv.at[GA_BACK])
    local = dot3(split(back_in[...].T), pair(inverse))[:sd]
    h = pm * (kin_ref[...] * w + local)
    hw[...] = h

    def send_late(other):
        push(hw.at[seat_rows(other)], late.at[seat_rows(seat)], LATE, (team + other, g))

    each_mate(send_late)
    late[seat_rows(seat), :] = hw[seat_rows(seat), :]

    h_out[0, :, :n] = jnp.where(real_lane, h, 0.0)
    h_out[0, :, n:] = jnp.where(real_lane, swap(h), 0.0)

    wait_rows(late, (TEAM - 1) * part, recv.at[LATE])
    found = gram(jnp.concatenate([late[pl.ds(r, TEAM, stride=part), :] for r in range(part)], axis=1),
                 ss_high[...], ss_low[...])
    for t in range(TEAM):
        late_part[t, :, :size] = found[t:t + 1]

    def send_part(p):
        push(late_part, late_in.at[g], LATE_GA, (b, p))

    each(ng, g, send_part)
    late_in[g] = late_part[...]

    wait_rows(early_ga, ng - 1, recv.at[EARLY_GA])
    early_all[b] = jnp.sum(early_ga[...], axis=0)

    def send_early_all(p):
        push(early_all.at[b], early_all.at[b], EARLY_BAND, (p, g))

    each(nb, b, send_early_all)


    wait_rows(late_in, ng - 1, recv.at[LATE_GA])
    late_all[b] = jnp.sum(late_in[...], axis=0)

    def send_whole(p):
        push(late_all.at[b], late_all.at[b], LATE_BAND, (p, g))

    each(nb, b, send_whole)

    wait_rows(early_all, nb - 1, recv.at[EARLY_BAND])

    def early_rows(a):
        return jnp.concatenate([early_all[p, a] for p in range(nb)], axis=0)[:, :size]

    def full(top):
        return jnp.concatenate(
            [top, jnp.concatenate([-top[:, width:2 * width], top[:, :width]], axis=1)], axis=0)

    big_a[...] = full(jnp.concatenate([early_rows(a) for a in range(2, 5)], axis=0))
    here = lax.broadcasted_iota(jnp.int32, (size, size), 0)
    there = lax.broadcasted_iota(jnp.int32, (size, size), 1)
    big_b[...] = jnp.where(here == there, 1.0, 0.0).astype(F32)
    row_id = lax.broadcasted_iota(jnp.int32, (size, 1), 0)
    col_id = lax.broadcasted_iota(jnp.int32, (1, size), 1)

    deep = 4

    def eliminate(i, carry):
        j = i * deep
        row = [big_a[pl.ds(j + m, 1), :] for m in range(deep)]
        inv_row = [big_b[pl.ds(j + m, 1), :] for m in range(deep)]
        a, inv = big_a[...], big_b[...]
        pivots = [[jnp.sum(jnp.where(col_id == j + q, row[m], 0.0), axis=1, keepdims=True) if q >= m else None
                   for q in range(deep)] for m in range(deep)]
        column = [jnp.sum(jnp.where(col_id == j + m, a, 0.0), axis=1, keepdims=True) for m in range(deep)]
        for m in range(deep):
            scale = 1.0 / pivots[m][m]
            for q in range(m + 1, deep):
                factor = pivots[m][q] * scale
                row[q] = row[q] - factor * row[m]
                inv_row[q] = inv_row[q] - factor * inv_row[m]
                column[q] = column[q] - factor * column[m]
                for t in range(q, deep):
                    pivots[q][t] = pivots[q][t] - factor * pivots[m][t]
            below = jnp.where(row_id > j + m, column[m], 0.0)
            a = a - below * (row[m] * scale)
            inv = inv - below * (inv_row[m] * scale)
        big_a[...] = a
        big_b[...] = inv
        return carry

    lax.fori_loop(0, size // deep, eliminate, 0)
    diag = jnp.sum(jnp.where(here == there, big_a[...], 0.0), axis=1, keepdims=True)
    lower_inv = big_b[...] / jnp.sqrt(diag)

    wait_rows(late_all, nb - 1, recv.at[LATE_BAND])
    late_gram = []
    for first in range(0, nb, TEAM):
        total = late_all[first]
        for t in range(1, TEAM):
            total = total + late_all[first + t]
        late_gram += [total[t] for t in range(TEAM)]
    late_gram = jnp.concatenate(late_gram, axis=0)
    top = jnp.concatenate([early_rows(0), late_gram[:, :size], early_rows(1)], axis=0)
    red_out[...] = dot(dot(lower_inv, full(top), NT), lower_inv, NT)

    wait_rows(ga_in, (ng - 1) * rb, send.at[GA_OUT])
    wait_rows(back_in, (ng - 1) * rb, send.at[GA_BACK])

    wait_for(share.at[:, pl.ds(0, (nb - 1) * part)], send.at[GROUP])
    wait_rows(rows_src, 2 * (TEAM - 1) * part, send.at[MATES])
    wait_rows(early_in, TEAM - 1, send.at[EARLY])
    wait_rows(early_ga, ng - 1, send.at[EARLY_GA])
    wait_rows(early_all, nb - 1, send.at[EARLY_BAND])
    wait_rows(late, (TEAM - 1) * part, send.at[LATE])
    wait_rows(late_in, ng - 1, send.at[LATE_GA])
    wait_rows(late_all, nb - 1, send.at[LATE_BAND])


def solution(mesh):
    nb, ng = mesh.shape["band"], mesh.shape["ga"]

    def shards(coef_x, coef_w, coef_p, hcoef_x, hcoef_p, potential, stick_column, sphere_mask):
        n = potential.shape[1]
        planes = potential.shape[0]
        sd = sphere_mask.shape[0]
        sp = n
        rb = 2 * planes
        half = n // 2
        cols = stick_column.reshape(ng * sd // n, n)
        size = 6 * nb
        part = sd // TEAM
        vmem = lambda *shape: pltpu.VMEM(shape, F32)
        scratch = [
            vmem(5, sd, n), vmem(2 * n, sp), vmem(2 * n, sp), pltpu.VMEM((ng, 2 * half, sp), BF16),
            vmem(2 * n, sp), vmem(2 * n, sp), vmem(3, nb * part, n), vmem(5 * TEAM * part, n),
            pltpu.VMEM((size, part * n), BF16),
            pltpu.VMEM((size, part * n), BF16), vmem(TEAM, 5, 1, LANES), vmem(TEAM, 5, 1, LANES),
            vmem(5, 1, LANES), vmem(ng, 5, 1, LANES), vmem(nb, 5, 1, LANES),
            vmem(sd, n), vmem(TEAM * part, n), vmem(TEAM, 1, LANES),
            vmem(ng, TEAM, 1, LANES), vmem(nb, TEAM, 1, LANES), vmem(size, size), vmem(size, size), vmem(sd, n),
            pltpu.VMEM((4, ng // 4, n), jnp.int32),
            pltpu.SemaphoreType.DMA((10,)), pltpu.SemaphoreType.DMA((10,)), pltpu.SemaphoreType.DMA((15,)),
        ]
        forward, inverse, z_plus, y_plus, y_minus, z_minus, fx2 = [jnp.asarray(t) for t in tables(n, planes)]
        args = [coef_w, sphere_mask, forward, hcoef_x, hcoef_p, coef_x, coef_p, cols, fx2,
                z_plus, y_plus, potential, y_minus, z_minus, inverse]
        scratch = [pltpu.VMEM(a.shape, a.dtype) for a in args] + scratch
        return pl.pallas_call(
            functools.partial(kernel, n, nb, ng, sd, planes),
            out_shape=[jax.ShapeDtypeStruct(coef_w.shape, F32), jax.ShapeDtypeStruct((size, size), F32)],
            in_specs=[pl.BlockSpec(memory_space=pltpu.HBM)] * len(args),
            out_specs=[pl.BlockSpec(memory_space=pltpu.VMEM)] * 2,
            scratch_shapes=scratch,
            compiler_params=pltpu.CompilerParams(
                collective_id=0, has_side_effects=True, vmem_limit_bytes=60 * 1024 * 1024),
        )(*args)

    vec = P("band", "ga", None)
    in_specs = (vec, vec, vec, vec, vec, P("ga", None, None), P(), P("ga", None))
    return jax.shard_map(shards, mesh=mesh, in_specs=in_specs, out_specs=(vec, P()), check_vma=False)
```

time: 66.5 us -> 56.3 us (0.85)
  Pallas kernels: 63.5 us -> 53.3 us
    pallas_call x1, Pallas kernels: 63.5 us -> 53.3 us  [shards(): pl.pallas_call(functools.partial(kernel, n, nb, ng, sd, planes), out_shap...]
where the time goes in v2:
time: 56.3 us; the launch traced here: 56.1 us
  Pallas kernels  53.3 us (95%)
  local copies, waits for them, and re-layouts  2.18 us (4%)
  between operations  0.65 us (1%)
    pallas_call x1, Pallas kernels, shards(): pl.pallas_call(functools.partial(kernel, n, nb, ng, sd, planes), out_shap...  53.3 us
    unnamed x4, local copies, waits for them, and re-layouts  2.18 us

profile of v2, /device:TPU:1, one launch (start us, length us, event | category | flops | bytes accessed | tf_op | source)
XLA Modules:
  0.0 56.1 jit_solution(13649003553275378769)
XLA Ops:
  0.6 53.3 %shard_map.158 = (f32[1,96,256]{2,1,0:T(8,128)}, f32[96,96]{1,0:T(8,128)}) custom-call(f32[1,96,256]{2,1,0:T(8,128)} %coef_w_in.1, s32[96,128]{1,0:T(8,128)} %mask_in.1, bf16[2,256,128]{2,1,0:T(8,128)(2,1)} %constant.14.clone.forward_in, f32[1,96,256]{2,1,0:T(8,128)} %hcoef_x_in.1, f32[1,96,256]{2,1,0:T(8,128)} %hcoef_p_in.1, f32[1,96,256]{2,1,0:T(8,128)} %coef_x_in.1, ...), custom_call_target="tpu_custom_call" | custom-call | tf_op jit(solution)/shard_map/pallas_call | solution.py:472
  54.0 0.0 copy-start
  54.0 1.6 %copy.19 = f32[1,96,256]{2,1,0:T(8,128)} copy(f32[1,96,256]{2,1,0:T(8,128)} %get-tuple-element.4) | data formatting | bytes 196608
  55.5 0.0 copy-done
  55.5 0.6 %copy.20 = f32[96,96]{1,0:T(8,128)} copy(f32[96,96]{1,0:T(8,128)S(1)} %copy-done) | data formatting | bytes 73728
Async XLA Ops:
  54.0 1.6 %copy-start = (f32[96,96]{1,0:T(8,128)S(1)}, f32[96,96]{1,0:T(8,128)}, u32[]{:S(2)}) copy-start(f32[96,96]{1,0:T(8,128)} %get-tuple-element.5) | copy-start | bytes 110596

commit v3 on v2

--- a/solution.py
+++ b/solution.py
@@ -17,8 +17,9 @@
 LANES = 128
 NT = (((1,), (1,)), ((), ()))
 NN = (((1,), (0,)), ((), ()))
-GA_OUT, GA_BACK, GROUP, MATES, EARLY, EARLY_GA, EARLY_BAND, LATE, LATE_GA, LATE_BAND = range(10)
+GA_OUT, GA_BACK, GROUP, RELAY, MATES, EARLY, EARLY_GA, EARLY_BAND, LATE, LATE_GA, LATE_BAND = range(11)
 TEAM = 4
+ROW = 4
 
 
 def dot(a, b, dims=NN, precision=HI):
@@ -71,11 +72,12 @@
            coef_w, mask, forward, hcoef_x, hcoef_p, coef_x, coef_p, cols, fx2,
            z_plus, y_plus, pot, y_minus, z_minus, inverse,
            src, ga_src, ga_in, hot, back_src, back_in, share, rows_src, ss_high, ss_low, early, early_in,
-           early_mine, early_ga, early_all, hw, late, late_part, late_in, late_all, big_a, big_b, kin_ref, q_cols, send, recv, load):
+           early_mine, early_ga, early_all, hw, late, late_part, late_in, late_all, big_a, big_b, kin_ref, q_cols, h_held, red_held, send, recv, load, near, store):
     half, quarter = n // 2, n // 4
     rb = 2 * planes
     sp = hot.shape[2]
-    cells = rb * half
+    few = half // 4
+    cells = rb * few
     width = 3 * nb
     size = 2 * width
     part = sd // TEAM
@@ -104,9 +106,10 @@
             return carry
         lax.fori_loop(0, count - 1, step, 0)
 
-    def push(src_ref, dst_ref, phase, where):
+    def push(src_ref, dst_ref, phase, where, landed=None):
         pltpu.make_async_remote_copy(
-            src_ref=src_ref, dst_ref=dst_ref, send_sem=send.at[phase], recv_sem=recv.at[phase],
+            src_ref=src_ref, dst_ref=dst_ref, send_sem=send.at[phase],
+            recv_sem=recv.at[phase] if landed is None else landed,
             device_id=where, device_id_type=pl.DeviceIdType.MESH).start()
 
     def wait_for(piece, sem):
@@ -163,7 +166,7 @@
     pl.semaphore_wait(barrier, ng + nb - 2)
 
     def send_ga(p):
-        push(ga_src.at[rows(p, rb)], ga_in.at[rows(g, rb)], GA_OUT, (b, p))
+        push(ga_src.at[rows(p, rb)], ga_in.at[rows(g, rb)], GA_OUT, (b, p), near.at[g // ROW])
 
     each(ng, g, send_ga)
     ga_in[rows(g, rb), :] = ga_src[rows(g, rb), :]
@@ -178,10 +181,19 @@
     def seat_rows(p):
         return pl.ds(pl.multiple_of(p * part, ROWS), part)
 
+    chips = nb // 2
+    chip, core = b // 2, lax.rem(b, 2)
+
+    def chip_at(step):
+        return lax.rem(chip + step + chips, chips)
+
     def send_group(p):
         push(src.at[pl.ds(2, 3), seat_rows(lax.rem(p, TEAM))], share.at[:, seat_rows(b)], GROUP, (p, g))
 
-    each(nb, b, send_group)
+    for step in (2, -2, 1, -1):
+        for c in range(2):
+            send_group(2 * chip_at(step) + c)
+    send_group(2 * chip + 1 - core)
     share[:, seat_rows(b), :] = src[2:5, seat_rows(seat), :]
 
     def each_mate(body):
@@ -197,6 +209,9 @@
     each_mate(send_mate)
     for a in range(2):
         rows_src[seat_rows(a * TEAM + seat), :] = src[a, seat_rows(seat), :]
+
+    def y_of(q):
+        return (cols_of(q) // n) & (half - 1)
 
     for copy in loads[7:9]:
         copy.wait()
@@ -213,9 +228,8 @@
         return q_cols[lax.rem(q, 4), pl.ds(q // 4, 1), :]
 
     def make_hot(q, carry):
-        zc = cols_of(q) & (half - 1)
-        one = jnp.where(lax.broadcasted_iota(jnp.int32, (half, sp), 0) == zc, 1.0, 0.0).astype(BF16)
-        hot[q] = jnp.concatenate([one, one], axis=0)
+        key = y_of(q) // few * half + (cols_of(q) & (half - 1))
+        hot[q] = jnp.where(lax.broadcasted_iota(jnp.int32, (4 * half, sp), 0) == key, 1.0, 0.0).astype(BF16)
         return carry
 
     lax.fori_loop(0, ng, make_hot, 0)
@@ -228,30 +242,44 @@
     radial = jnp.broadcast_to((fy * fy + fz * fz).astype(F32), (n, sp)).T[:sd]
     kin_ref[...] = 0.5 * (2.0 * math.pi / n) ** 2 * (fx2[...] + radial)
 
-    wait_rows(ga_in, (ng - 1) * rb, recv.at[GA_OUT])
+    nz = ng // ROW
+    mz = g // ROW
+
+    def row_at(i):
+        return lax.rem(mz + (i + 1) // 2 * (2 * lax.rem(i, 2) - 1) + nz, nz)
+
 
     def y_hot(q):
-        yc = (cols_of(q) // n) & (half - 1)
-        return lax.broadcasted_iota(jnp.int32, (half, sp), 0) == yc
-
-    group = 4 if ng % 4 == 0 else 2
+        return lax.broadcasted_iota(jnp.int32, (few, sp), 0) == (y_of(q) & (few - 1))
 
     def scatter(i, acc):
-        left, right = [], []
-        for t in range(group):
-            q = i * group + t
+        z = row_at(i)
+        if isinstance(i, int):
+            wait_rows(ga_in, (ROW - 1) * rb, near.at[z])
+        else:
+            wait_rows(ga_in, ROW * rb, near.at[z])
+        upper, lower, right = [], [], []
+        for t in range(ROW):
+            q = z * ROW + t
             v = ga_in[rows(q, rb), :]
             high = v.astype(BF16).astype(F32)
-            low = v - high
             here = y_hot(q)[None]
-            one = hot[q][:half]
-            for piece in (high, low):
-                spreadout = jnp.where(here, piece[:, None, :], 0.0).reshape(cells, sp)
-                left.append(spreadout.astype(BF16))
-                right.append(one)
-        return acc + dot(jnp.concatenate(left, axis=1), jnp.concatenate(right, axis=1), NT, None)
-
-    grid = lax.fori_loop(0, ng // group, scatter, jnp.zeros((cells, half), F32))
+            for piece, part_of in ((high, upper), (v - high, lower)):
+                part_of.append(jnp.where(here, piece[:, None, :], 0.0).reshape(cells, sp).astype(BF16))
+            right.append(hot[q])
+        left = jnp.concatenate([jnp.concatenate(upper, axis=1), jnp.concatenate(lower, axis=1)], axis=0)
+        return acc + dot(left, jnp.concatenate(right, axis=1), NT, None)
+
+    grid = lax.fori_loop(1, nz, scatter, scatter(0, jnp.zeros((2 * cells, 4 * half), F32)))
+    grid = grid[:cells] + grid[cells:]
+    grid = jnp.concatenate(
+        [grid[:, u * half:(u + 1) * half].reshape(rb, few, half) for u in range(4)], axis=1).reshape(rb * half, half)
+
+    wait_for(share.at[:, pl.ds(0, 9 * part)], recv.at[GROUP])
+    for way, last in ((1, 0), (-1, 1)):
+        near_pair = pl.ds(pl.multiple_of(2 * chip_at(-way) * part, ROWS), 2 * part)
+        for held_rows in (near_pair, seat_rows(2 * chip_at(-2 * way) + last)):
+            push(share.at[:, held_rows], share.at[:, held_rows], RELAY, (2 * chip_at(2 * way) + core, g))
 
     for copy in loads[9:]:
         copy.wait()
@@ -271,17 +299,21 @@
          for j in range(planes)], axis=0)
     product = dot3(split(product), pair(z_minus))
     product = jnp.concatenate([product[:, :n], product[:, n:]], axis=0)
-    high = product.astype(BF16).astype(F32)
-    low = product - high
-    both = jnp.where(lax.broadcasted_iota(jnp.int32, (1, n), 1) < half, high, low).astype(BF16)
+    product = product.reshape(rb, 4, few, 2 * half)
+    left_lanes = lax.broadcasted_iota(jnp.int32, (1, n), 1) < half
+    product = jnp.concatenate(
+        [jnp.where(left_lanes, product[:, u].reshape(cells, n), product[:, u + 1].reshape(cells, n)) for u in (0, 2)],
+        axis=1)
+    both = jnp.concatenate(split(product), axis=0)
 
     def gather(i, carry):
-        pair = jnp.concatenate([hot[2 * i], hot[2 * i + 1]], axis=1)
-        found = dot(both, pair, NN, None)
+        first = row_at(nz - 1 - i // 2) * ROW + 2 * lax.rem(i, 2)
+        found = dot(both, jnp.concatenate([hot[first], hot[first + 1]], axis=1), NN, None)
+        found = found[:cells] + found[cells:]
         for t in range(2):
-            q = 2 * i + t
+            q = first + t
             here = y_hot(q)[None]
-            part = found[:, t * sp:(t + 1) * sp].reshape(rb, half, sp)
+            part = found[:, t * sp:(t + 1) * sp].reshape(rb, few, sp)
             back_src[rows(q, rb), :] = jnp.sum(jnp.where(here, part, 0.0), axis=1)
 
             @pl.when(q != g)
@@ -292,7 +324,7 @@
     lax.fori_loop(0, ng // 2, gather, 0)
     back_in[rows(g, rb), :] = back_src[rows(g, rb), :]
 
-    wait_for(share.at[:, pl.ds(0, (nb - 1) * part)], recv.at[GROUP])
+    wait_for(share.at[:, pl.ds(0, 6 * part)], recv.at[RELAY])
 
     def make_span(i, carry):
         for t in range(3):
@@ -319,14 +351,6 @@
 
     each_mate(send_early)
     early_in[seat] = early[seat]
-    wait_rows(early_in, TEAM - 1, recv.at[EARLY])
-    early_mine[...] = jnp.sum(early_in[...], axis=0)
-
-    def send_mine(p):
-        push(early_mine, early_ga.at[g], EARLY_GA, (b, p))
-
-    each(ng, g, send_mine)
-    early_ga[g] = early_mine[...]
     wait_rows(back_in, (ng - 1) * rb, recv.at[GA_BACK])
     local = dot3(split(back_in[...].T), pair(inverse))[:sd]
     h = pm * (kin_ref[...] * w + local)
@@ -338,9 +362,19 @@
     each_mate(send_late)
     late[seat_rows(seat), :] = hw[seat_rows(seat), :]
 
-    h_out[0, :, :n] = jnp.where(real_lane, h, 0.0)
-    h_out[0, :, n:] = jnp.where(real_lane, swap(h), 0.0)
-
+    h_held[0, :, :n] = jnp.where(real_lane, h, 0.0)
+    h_held[0, :, n:] = jnp.where(real_lane, swap(h), 0.0)
+    store_h = pltpu.make_async_copy(h_held, h_out, store.at[0])
+    store_h.start()
+
+    wait_rows(early_in, TEAM - 1, recv.at[EARLY])
+    early_mine[...] = jnp.sum(early_in[...], axis=0)
+
+    def send_mine(p):
+        push(early_mine, early_ga.at[g], EARLY_GA, (b, p))
+
+    each(ng, g, send_mine)
+    early_ga[g] = early_mine[...]
     wait_rows(late, (TEAM - 1) * part, recv.at[LATE])
     found = gram(jnp.concatenate([late[pl.ds(r, TEAM, stride=part), :] for r in range(part)], axis=1),
                  ss_high[...], ss_low[...])
@@ -386,13 +420,13 @@
     row_id = lax.broadcasted_iota(jnp.int32, (size, 1), 0)
     col_id = lax.broadcasted_iota(jnp.int32, (1, size), 1)
 
-    deep = 4
-
-    def eliminate(i, carry):
-        j = i * deep
+    deep = 8
+
+    def eliminate(top, i, carry):
+        j = top + i * deep
         row = [big_a[pl.ds(j + m, 1), :] for m in range(deep)]
         inv_row = [big_b[pl.ds(j + m, 1), :] for m in range(deep)]
-        a, inv = big_a[...], big_b[...]
+        a, inv = big_a[top:, :], big_b[top:, :]
         pivots = [[jnp.sum(jnp.where(col_id == j + q, row[m], 0.0), axis=1, keepdims=True) if q >= m else None
                    for q in range(deep)] for m in range(deep)]
         column = [jnp.sum(jnp.where(col_id == j + m, a, 0.0), axis=1, keepdims=True) for m in range(deep)]
@@ -405,14 +439,16 @@
                 column[q] = column[q] - factor * column[m]
                 for t in range(q, deep):
                     pivots[q][t] = pivots[q][t] - factor * pivots[m][t]
-            below = jnp.where(row_id > j + m, column[m], 0.0)
+            below = jnp.where(row_id[top:] > j + m, column[m], 0.0)
             a = a - below * (row[m] * scale)
             inv = inv - below * (inv_row[m] * scale)
-        big_a[...] = a
-        big_b[...] = inv
+        big_a[top:, :] = a
+        big_b[top:, :] = inv
         return carry
 
-    lax.fori_loop(0, size // deep, eliminate, 0)
+    stretch = size // 6
+    for top in range(0, size, stretch):
+        lax.fori_loop(0, stretch // deep, functools.partial(eliminate, top), 0)
     diag = jnp.sum(jnp.where(here == there, big_a[...], 0.0), axis=1, keepdims=True)
     lower_inv = big_b[...] / jnp.sqrt(diag)
 
@@ -425,12 +461,15 @@
         late_gram += [total[t] for t in range(TEAM)]
     late_gram = jnp.concatenate(late_gram, axis=0)
     top = jnp.concatenate([early_rows(0), late_gram[:, :size], early_rows(1)], axis=0)
-    red_out[...] = dot(dot(lower_inv, full(top), NT), lower_inv, NT)
-
+    red_held[...] = dot(dot(lower_inv, full(top), NT), lower_inv, NT)
+
+    store_red = pltpu.make_async_copy(red_held, red_out, store.at[1])
+    store_red.start()
     wait_rows(ga_in, (ng - 1) * rb, send.at[GA_OUT])
     wait_rows(back_in, (ng - 1) * rb, send.at[GA_BACK])
 
-    wait_for(share.at[:, pl.ds(0, (nb - 1) * part)], send.at[GROUP])
+    wait_for(share.at[:, pl.ds(0, 9 * part)], send.at[GROUP])
+    wait_for(share.at[:, pl.ds(0, 6 * part)], send.at[RELAY])
     wait_rows(rows_src, 2 * (TEAM - 1) * part, send.at[MATES])
     wait_rows(early_in, TEAM - 1, send.at[EARLY])
     wait_rows(early_ga, ng - 1, send.at[EARLY_GA])
@@ -438,6 +477,8 @@
     wait_rows(late, (TEAM - 1) * part, send.at[LATE])
     wait_rows(late_in, ng - 1, send.at[LATE_GA])
     wait_rows(late_all, nb - 1, send.at[LATE_BAND])
+    store_h.wait()
+    store_red.wait()
 
 
 def solution(mesh):
@@ -455,7 +496,7 @@
         part = sd // TEAM
         vmem = lambda *shape: pltpu.VMEM(shape, F32)
         scratch = [
-            vmem(5, sd, n), vmem(2 * n, sp), vmem(2 * n, sp), pltpu.VMEM((ng, 2 * half, sp), BF16),
+            vmem(5, sd, n), vmem(2 * n, sp), vmem(2 * n, sp), pltpu.VMEM((ng, 4 * half, sp), BF16),
             vmem(2 * n, sp), vmem(2 * n, sp), vmem(3, nb * part, n), vmem(5 * TEAM * part, n),
             pltpu.VMEM((size, part * n), BF16),
             pltpu.VMEM((size, part * n), BF16), vmem(TEAM, 5, 1, LANES), vmem(TEAM, 5, 1, LANES),
@@ -463,7 +504,9 @@
             vmem(sd, n), vmem(TEAM * part, n), vmem(TEAM, 1, LANES),
             vmem(ng, TEAM, 1, LANES), vmem(nb, TEAM, 1, LANES), vmem(size, size), vmem(size, size), vmem(sd, n),
             pltpu.VMEM((4, ng // 4, n), jnp.int32),
-            pltpu.SemaphoreType.DMA((10,)), pltpu.SemaphoreType.DMA((10,)), pltpu.SemaphoreType.DMA((15,)),
+            vmem(1, sd, 2 * n), vmem(size, size),
+            pltpu.SemaphoreType.DMA((11,)), pltpu.SemaphoreType.DMA((11,)), pltpu.SemaphoreType.DMA((15,)),
+            pltpu.SemaphoreType.DMA((ng // ROW,)), pltpu.SemaphoreType.DMA((2,)),
         ]
         forward, inverse, z_plus, y_plus, y_minus, z_minus, fx2 = [jnp.asarray(t) for t in tables(n, planes)]
         args = [coef_w, sphere_mask, forward, hcoef_x, hcoef_p, coef_x, coef_p, cols, fx2,
@@ -473,7 +516,7 @@
             functools.partial(kernel, n, nb, ng, sd, planes),
             out_shape=[jax.ShapeDtypeStruct(coef_w.shape, F32), jax.ShapeDtypeStruct((size, size), F32)],
             in_specs=[pl.BlockSpec(memory_space=pltpu.HBM)] * len(args),
-            out_specs=[pl.BlockSpec(memory_space=pltpu.VMEM)] * 2,
+            out_specs=[pl.BlockSpec(memory_space=pltpu.HBM)] * 2,
             scratch_shapes=scratch,
             compiler_params=pltpu.CompilerParams(
                 collective_id=0, has_side_effects=True, vmem_limit_bytes=60 * 1024 * 1024),

time: 56.3 us -> 54.4 us (0.966)
  Pallas kernels: 53.3 us -> 51.4 us
    pallas_call x1, Pallas kernels: 53.3 us -> 51.4 us  [shards(): pl.pallas_call(functools.partial(kernel, n, nb, ng, sd, planes), out_shap...]
where the time goes in v3:
time: 54.4 us; the launch traced here: 54.2 us
  Pallas kernels  51.4 us (94%)
  local copies, waits for them, and re-layouts  2.18 us (4%)
  between operations  0.65 us (1%)
    pallas_call x1, Pallas kernels, shards(): pl.pallas_call(functools.partial(kernel, n, nb, ng, sd, planes), out_shap...  51.4 us
    unnamed x4, local copies, waits for them, and re-layouts  2.18 us

profile of v3, /device:TPU:1, one launch (start us, length us, event | category | flops | bytes accessed | tf_op | source)
XLA Modules:
  0.0 54.2 jit_solution(11075591583982002858)
XLA Ops:
  0.6 51.4 %shard_map.158 = (f32[1,96,256]{2,1,0:T(8,128)}, f32[96,96]{1,0:T(8,128)}) custom-call(f32[1,96,256]{2,1,0:T(8,128)} %coef_w_in.1, s32[96,128]{1,0:T(8,128)} %mask_in.1, bf16[2,256,128]{2,1,0:T(8,128)(2,1)} %constant.14.clone.forward_in, f32[1,96,256]{2,1,0:T(8,128)} %hcoef_x_in.1, f32[1,96,256]{2,1,0:T(8,128)} %hcoef_p_in.1, f32[1,96,256]{2,1,0:T(8,128)} %coef_x_in.1, ...), custom_call_target="tpu_custom_call" | custom-call | tf_op jit(solution)/shard_map/pallas_call | solution.py:515
  52.0 0.0 copy-start
  52.0 1.6 %copy.19 = f32[1,96,256]{2,1,0:T(8,128)} copy(f32[1,96,256]{2,1,0:T(8,128)} %get-tuple-element.4) | data formatting | bytes 196608
  53.6 0.0 copy-done
  53.6 0.6 %copy.20 = f32[96,96]{1,0:T(8,128)} copy(f32[96,96]{1,0:T(8,128)S(1)} %copy-done) | data formatting | bytes 73728
Async XLA Ops:
  52.0 1.6 %copy-start = (f32[96,96]{1,0:T(8,128)S(1)}, f32[96,96]{1,0:T(8,128)}, u32[]{:S(2)}) copy-start(f32[96,96]{1,0:T(8,128)} %get-tuple-element.5) | copy-start | bytes 110596

commit v4 on v3

--- a/solution.py
+++ b/solution.py
@@ -163,14 +163,6 @@
     src[3] = w
     wide = jnp.concatenate([w, jnp.zeros((sp - sd, n), F32)], axis=0) if sp > sd else w
     ga_src[...] = dot3(pair(forward), split(wide), NT)
-    pl.semaphore_wait(barrier, ng + nb - 2)
-
-    def send_ga(p):
-        push(ga_src.at[rows(p, rb)], ga_in.at[rows(g, rb)], GA_OUT, (b, p), near.at[g // ROW])
-
-    each(ng, g, send_ga)
-    ga_in[rows(g, rb), :] = ga_src[rows(g, rb), :]
-
     for copy in loads[3:7]:
         copy.wait()
     src[0] = pack(hcoef_x) * pm
@@ -178,6 +170,8 @@
     src[2] = pack(coef_x) * pm
     src[4] = pack(coef_p) * pm
 
+    pl.semaphore_wait(barrier, ng + nb - 2)
+
     def seat_rows(p):
         return pl.ds(pl.multiple_of(p * part, ROWS), part)
 
@@ -195,6 +189,12 @@
             send_group(2 * chip_at(step) + c)
     send_group(2 * chip + 1 - core)
     share[:, seat_rows(b), :] = src[2:5, seat_rows(seat), :]
+
+    def send_ga(p):
+        push(ga_src.at[rows(p, rb)], ga_in.at[rows(g, rb)], GA_OUT, (b, p), near.at[g // ROW])
+
+    each(ng, g, send_ga)
+    ga_in[rows(g, rb), :] = ga_src[rows(g, rb), :]
 
     def each_mate(body):
         def step(d, carry):
@@ -450,7 +450,8 @@
     for top in range(0, size, stretch):
         lax.fori_loop(0, stretch // deep, functools.partial(eliminate, top), 0)
     diag = jnp.sum(jnp.where(here == there, big_a[...], 0.0), axis=1, keepdims=True)
-    lower_inv = big_b[...] / jnp.sqrt(diag)
+    lower_inv = split(big_b[...] / jnp.sqrt(diag))
+    h_x, h_p = early_rows(0), early_rows(1)
 
     wait_rows(late_all, nb - 1, recv.at[LATE_BAND])
     late_gram = []
@@ -460,8 +461,8 @@
             total = total + late_all[first + t]
         late_gram += [total[t] for t in range(TEAM)]
     late_gram = jnp.concatenate(late_gram, axis=0)
-    top = jnp.concatenate([early_rows(0), late_gram[:, :size], early_rows(1)], axis=0)
-    red_held[...] = dot(dot(lower_inv, full(top), NT), lower_inv, NT)
+    top = jnp.concatenate([h_x, late_gram[:, :size], h_p], axis=0)
+    red_held[...] = dot3(split(dot3(lower_inv, split(full(top)), NT)), lower_inv, NT)
 
     store_red = pltpu.make_async_copy(red_held, red_out, store.at[1])
     store_red.start()

time: 54.4 us -> 53.6 us (0.985)
  Pallas kernels: 51.4 us -> 50.6 us
    pallas_call x1, Pallas kernels: 51.4 us -> 50.6 us  [shards(): pl.pallas_call(functools.partial(kernel, n, nb, ng, sd, planes), out_shap...]
where the time goes in v4:
time: 53.6 us; the launch traced here: 53.4 us
  Pallas kernels  50.6 us (94%)
  local copies, waits for them, and re-layouts  2.18 us (4%)
  between operations  0.65 us (1%)
    pallas_call x1, Pallas kernels, shards(): pl.pallas_call(functools.partial(kernel, n, nb, ng, sd, planes), out_shap...  50.6 us
    unnamed x4, local copies, waits for them, and re-layouts  2.18 us

profile of v4, /device:TPU:1, one launch (start us, length us, event | category | flops | bytes accessed | tf_op | source)
XLA Modules:
  0.0 53.4 jit_solution(8875010465249385449)
XLA Ops:
  0.6 50.6 %shard_map.158 = (f32[1,96,256]{2,1,0:T(8,128)}, f32[96,96]{1,0:T(8,128)}) custom-call(f32[1,96,256]{2,1,0:T(8,128)} %coef_w_in.1, s32[96,128]{1,0:T(8,128)} %mask_in.1, bf16[2,256,128]{2,1,0:T(8,128)(2,1)} %constant.14.clone.forward_in, f32[1,96,256]{2,1,0:T(8,128)} %hcoef_x_in.1, f32[1,96,256]{2,1,0:T(8,128)} %hcoef_p_in.1, f32[1,96,256]{2,1,0:T(8,128)} %coef_x_in.1, ...), custom_call_target="tpu_custom_call" | custom-call | tf_op jit(solution)/shard_map/pallas_call | solution.py:516
  51.2 0.0 copy-start
  51.2 1.6 %copy.19 = f32[1,96,256]{2,1,0:T(8,128)} copy(f32[1,96,256]{2,1,0:T(8,128)} %get-tuple-element.4) | data formatting | bytes 196608
  52.8 0.0 copy-done
  52.8 0.6 %copy.20 = f32[96,96]{1,0:T(8,128)} copy(f32[96,96]{1,0:T(8,128)S(1)} %copy-done) | data formatting | bytes 73728
Async XLA Ops:
  51.2 1.6 %copy-start = (f32[96,96]{1,0:T(8,128)S(1)}, f32[96,96]{1,0:T(8,128)}, u32[]{:S(2)}) copy-start(f32[96,96]{1,0:T(8,128)} %get-tuple-element.5) | copy-start | bytes 110596

commit v5 on v4

--- a/solution.py
+++ b/solution.py
@@ -71,7 +71,7 @@
            h_out, red_out,
            coef_w, mask, forward, hcoef_x, hcoef_p, coef_x, coef_p, cols, fx2,
            z_plus, y_plus, pot, y_minus, z_minus, inverse,
-           src, ga_src, ga_in, hot, back_src, back_in, share, rows_src, ss_high, ss_low, early, early_in,
+           src, ga_src, ga_in, hot, back_src, back_in, share, rows_src, ss, early, early_in,
            early_mine, early_ga, early_all, hw, late, late_part, late_in, late_all, big_a, big_b, kin_ref, q_cols, h_held, red_held, send, recv, load, near, store):
     half, quarter = n // 2, n // 4
     rb = 2 * planes
@@ -128,11 +128,10 @@
     def pair(table):
         return table[0], table[1]
 
-    def gram(left, s_high, s_low):
+    def gram(left):
         count = left.shape[0]
-        high, low = split(left)
-        upper = dot(jnp.concatenate([high, low], axis=0), s_high, NT, None)
-        return upper[:count] + upper[count:] + dot(high, s_low, NT, None)
+        found = dot(jnp.concatenate(split(left), axis=0), ss[...], NT, None)
+        return found[:count, :size] + found[count:, :size] + found[:count, size:]
 
     held = [coef_w, mask, forward, hcoef_x, hcoef_p, coef_x, coef_p, cols, fx2,
             z_plus, y_plus, pot, y_minus, z_minus, inverse]
@@ -332,16 +331,15 @@
             s = jnp.concatenate([share[a, pl.ds(r, nb, stride=part), :] for a in range(3)], axis=0)
             high, low = split(jnp.concatenate([s, swap(s) * sign], axis=0))
             at = pl.ds(pl.multiple_of(r * n, n), n)
-            ss_high[:, at] = high
-            ss_low[:, at] = low
+            ss[:size, at] = high
+            ss[size:, at] = low
         return carry
 
     lax.fori_loop(0, part // 3, make_span, 0)
     wait_rows(rows_src, 2 * (TEAM - 1) * part, recv.at[MATES])
     for a in range(3):
         rows_src[(2 + a) * TEAM * part:(3 + a) * TEAM * part] = share[a, pl.ds(pl.multiple_of(team * part, ROWS), TEAM * part), :]
-    found = gram(jnp.concatenate([rows_src[pl.ds(r, 5 * TEAM, stride=part), :] for r in range(part)], axis=1),
-                 ss_high[...], ss_low[...])
+    found = gram(jnp.concatenate([rows_src[pl.ds(r, 5 * TEAM, stride=part), :] for r in range(part)], axis=1))
     for t in range(TEAM):
         for a in range(5):
             early[t, a, :, :size] = found[a * TEAM + t:a * TEAM + t + 1]
@@ -376,8 +374,7 @@
     each(ng, g, send_mine)
     early_ga[g] = early_mine[...]
     wait_rows(late, (TEAM - 1) * part, recv.at[LATE])
-    found = gram(jnp.concatenate([late[pl.ds(r, TEAM, stride=part), :] for r in range(part)], axis=1),
-                 ss_high[...], ss_low[...])
+    found = gram(jnp.concatenate([late[pl.ds(r, TEAM, stride=part), :] for r in range(part)], axis=1))
     for t in range(TEAM):
         late_part[t, :, :size] = found[t:t + 1]
 
@@ -499,8 +496,8 @@
         scratch = [
             vmem(5, sd, n), vmem(2 * n, sp), vmem(2 * n, sp), pltpu.VMEM((ng, 4 * half, sp), BF16),
             vmem(2 * n, sp), vmem(2 * n, sp), vmem(3, nb * part, n), vmem(5 * TEAM * part, n),
-            pltpu.VMEM((size, part * n), BF16),
-            pltpu.VMEM((size, part * n), BF16), vmem(TEAM, 5, 1, LANES), vmem(TEAM, 5, 1, LANES),
+            pltpu.VMEM((2 * size, part * n), BF16),
+            vmem(TEAM, 5, 1, LANES), vmem(TEAM, 5, 1, LANES),
             vmem(5, 1, LANES), vmem(ng, 5, 1, LANES), vmem(nb, 5, 1, LANES),
             vmem(sd, n), vmem(TEAM * part, n), vmem(TEAM, 1, LANES),
             vmem(ng, TEAM, 1, LANES), vmem(nb, TEAM, 1, LANES), vmem(size, size), vmem(size, size), vmem(sd, n),

time: 53.6 us -> 53.8 us (level)
  no operation moved by 1% of the time
where the time goes in v5:
time: 53.8 us; the launch traced here: 53.6 us
  Pallas kernels  50.8 us (94%)
  local copies, waits for them, and re-layouts  2.18 us (4%)
  between operations  0.65 us (1%)
    pallas_call x1, Pallas kernels, shards(): pl.pallas_call(functools.partial(kernel, n, nb, ng, sd, planes), out_shap...  50.8 us
    unnamed x4, local copies, waits for them, and re-layouts  2.18 us

profile of v5, /device:TPU:1, one launch (start us, length us, event | category | flops | bytes accessed | tf_op | source)
XLA Modules:
  0.0 53.6 jit_solution(9617732858938174700)
XLA Ops:
  0.6 50.8 %shard_map.158 = (f32[1,96,256]{2,1,0:T(8,128)}, f32[96,96]{1,0:T(8,128)}) custom-call(f32[1,96,256]{2,1,0:T(8,128)} %coef_w_in.1, s32[96,128]{1,0:T(8,128)} %mask_in.1, bf16[2,256,128]{2,1,0:T(8,128)(2,1)} %constant.14.clone.forward_in, f32[1,96,256]{2,1,0:T(8,128)} %hcoef_x_in.1, f32[1,96,256]{2,1,0:T(8,128)} %hcoef_p_in.1, f32[1,96,256]{2,1,0:T(8,128)} %coef_x_in.1, ...), custom_call_target="tpu_custom_call" | custom-call | tf_op jit(solution)/shard_map/pallas_call | solution.py:513
  51.4 0.0 copy-start
  51.4 1.6 %copy.19 = f32[1,96,256]{2,1,0:T(8,128)} copy(f32[1,96,256]{2,1,0:T(8,128)} %get-tuple-element.4) | data formatting | bytes 196608
  53.0 0.0 copy-done
  53.0 0.6 %copy.20 = f32[96,96]{1,0:T(8,128)} copy(f32[96,96]{1,0:T(8,128)S(1)} %copy-done) | data formatting | bytes 73728
Async XLA Ops:
  51.4 1.6 %copy-start = (f32[96,96]{1,0:T(8,128)S(1)}, f32[96,96]{1,0:T(8,128)}, u32[]{:S(2)}) copy-start(f32[96,96]{1,0:T(8,128)} %get-tuple-element.5) | copy-start | bytes 110596
